TPU v7x, 256 devices: a whole 4x4x8 slice. The times are simulated.
256 devices in a mesh: tm: 16 (over y_hi, z), space: 16 (over x, y_lo, core).
Axes of the slice: x: 4, y: 4 (y_hi: 2, y_lo: 2; y = y_hi * 2 + y_lo), z: 8, core: 2. Of those that a mesh axis runs over, the one named last changes fastest.
Arguments:
- query: bfloat16 [16, 16, 384, 1536], P('tm', 'space'), may hold values from -6 to 6
- fresh_key: bfloat16 [16, 16, 384, 1536], P('tm', 'space'), may hold values from -6 to 6
- fresh_value: bfloat16 [16, 16, 384, 1536], P('tm', 'space'), may hold values from -6 to 6
- stale_kv: bfloat16 [2, 16, 16, 384, 1536], P(None, 'tm', 'space'), may hold values from -6 to 6
- text_kv: bfloat16 [2, 256, 1536], P(None, 'space'), may hold values from -6 to 6
- window: int32 [12, 2], replicated, may hold values from 0 to 1, as said below
- text_len: int32 [1], replicated, may hold values from 64 to 256
Outputs:
- attended: bfloat16 [16, 16, 384, 1536], P('tm', 'space')
Inputs may be any that keep to these rules, and one draw needn't show every extreme that they name: `window`: each of the four pairs of reaches (0 or 1 along frames, 0 or 1 along space) belongs to exactly 3 heads.
All inputs are finite; a program needn't handle non-finite values.
Results may differ from a plain program's by a relative error of at most 0.0046.
Values may be sent and summed in bfloat16 or wider, within the bound.
A program may use at most 128 MiB of HBM per device.

v0:
```python
import math

import jax
import jax.numpy as jnp
from jax import lax
from jax.sharding import PartitionSpec as P


def extended(block, sides, width):
    for axis, dim in sides:
        count = lax.axis_size(axis)
        forward = [(i, i + 1) for i in range(count - 1)]
        backward = [(target, source) for source, target in forward]
        low = lax.ppermute(
            lax.slice_in_dim(block, block.shape[dim] - width, None, axis=dim), axis, forward
        )
        high = lax.ppermute(lax.slice_in_dim(block, 0, width, axis=dim), axis, backward)
        block = jnp.concatenate([low, block, high], axis=dim)
    return block


def attend_tile(query_rows, key_rows, value_rows, slot_valid, window, text_len):
    tile_rows = query_rows.shape[0]
    width = query_rows.shape[1]
    heads = window.shape[0]
    head_dim = width // heads
    scale = 1.0 / math.sqrt(head_dim)
    near_count = 9 * tile_rows
    text_rows = key_rows.shape[0] - near_count
    tile_of = jnp.arange(near_count, dtype=jnp.int32) // tile_rows
    step_time = tile_of // 3 - 1
    step_space = tile_of % 3 - 1
    tile_valid = slot_valid[tile_of]
    text_valid = jnp.arange(text_rows, dtype=jnp.int32) < text_len[0]
    query_heads = query_rows.reshape(tile_rows, heads, head_dim).transpose(1, 0, 2)
    key_heads = key_rows.reshape(-1, heads, head_dim).transpose(1, 0, 2)
    value_heads = value_rows.reshape(-1, heads, head_dim).transpose(1, 0, 2)

    def one_head(packed):
        query_head, key_head, value_head, reach = packed
        near_ok = tile_valid & (jnp.abs(step_time) <= reach[0]) & (jnp.abs(step_space) <= reach[1])
        allowed = jnp.concatenate([near_ok, text_valid])
        scores = jnp.dot(query_head, key_head.T, preferred_element_type=jnp.float32) * scale
        masked = jnp.where(allowed[None, :], scores, -1e30)
        peak = jnp.max(masked, axis=1, keepdims=True)
        weights = jnp.where(allowed[None, :], jnp.exp(masked - peak), 0.0)
        total = jnp.sum(weights, axis=1, keepdims=True)
        mixed = jnp.dot(
            weights.astype(jnp.bfloat16), value_head, preferred_element_type=jnp.float32
        )
        return mixed / total

    result = lax.map(one_head, (query_heads, key_heads, value_heads, window))
    return result.transpose(1, 0, 2).reshape(tile_rows, width).astype(jnp.bfloat16)


def tile_output(
    block,
    query_rows,
    key_here,
    value_here,
    time_pos,
    space_pos,
    time_tiles,
    space_tiles,
    text_both,
    window,
    text_len,
):
    tile_rows, width = query_rows.shape
    near_keys = (
        block[0].reshape(9, tile_rows, width).at[4].set(key_here).reshape(9 * tile_rows, width)
    )
    near_values = (
        block[1].reshape(9, tile_rows, width).at[4].set(value_here).reshape(9 * tile_rows, width)
    )
    key_rows = jnp.concatenate([near_keys, text_both[0]], axis=0)
    value_rows = jnp.concatenate([near_values, text_both[1]], axis=0)
    offsets = jnp.arange(3, dtype=jnp.int32) - 1
    time_ok = (time_pos + offsets >= 0) & (time_pos + offsets < time_tiles)
    space_ok = (space_pos + offsets >= 0) & (space_pos + offsets < space_tiles)
    slot_valid = (time_ok[:, None] & space_ok[None, :]).reshape(9)
    return attend_tile(query_rows, key_rows, value_rows, slot_valid, window, text_len)


def on_device(query, fresh_key, fresh_value, stale_kv, text_kv, window, text_len):
    text_both = lax.all_gather(text_kv, "space", axis=1, tiled=True)
    time_pos = lax.axis_index("tm")
    space_pos = lax.axis_index("space")
    nearby = extended(stale_kv, (("tm", 1), ("space", 2)), 1)
    result = tile_output(
        nearby,
        query[0, 0],
        fresh_key[0, 0],
        fresh_value[0, 0],
        time_pos,
        space_pos,
        lax.axis_size("tm"),
        lax.axis_size("space"),
        text_both,
        window,
        text_len,
    )
    return result[None, None]


def solution(mesh):
    in_specs = (
        P("tm", "space", None, None),
        P("tm", "space", None, None),
        P("tm", "space", None, None),
        P(None, "tm", "space", None, None),
        P(None, "space", None),
        P(),
        P(),
    )
    out_specs = P("tm", "space", None, None)
    return jax.shard_map(
        on_device, mesh=mesh, in_specs=in_specs, out_specs=out_specs, check_vma=False
    )
```

profile of v0, /device:TPU:1, one launch (start us, length us, event | category | flops | bytes accessed | tf_op | source)
XLA Modules:
  0.0 520.5 jit_solution(10104530315046647301)
XLA Ops:
  6.5 4.6 collective-permute-start
  12.5 48.8 %collective-permute-done = bf16[2,1,1,384,1536]{4,3,2,1,0:T(8,128)(2,1)S(1)} collective-permute-done((bf16[2,1,1,384,1536]{4,3,2,1,0:T(8,128)(2,1)}, bf16[2,1,1,384,1536]{4,3,2,1,0:T(8,128)(2,1)S(1)}, u32[]{:S(2)}, u32[]{:S(2)}) %collective-permute-start) | collective-permute-done | bytes 2359328 | tf_op jit(solution)/shard_map/ppermute | solution.py:14
  66.8 4.9 collective-permute-start.2
  71.7 3.0 collective-permute-start.3
  77.8 90.4 %all-gather.2.cloned.1.call-done = bf16[2,256,1536]{2,0,1:T(2,128)(2,1)} async-done(((bf16[2,16,1536]{2,0,1:T(2,128)(2,1)}), bf16[2,256,1536]{2,0,1:T(2,128)(2,1)}) %all-gather.2.cloned.1.call-update) | async-done | bytes 1572880 | tf_op jit(solution)/shard_map/all_gather | solution.py:87
  168.2 4.4 fusion.45
  172.6 2.9 copy.33
  179.7 51.8 %collective-permute-done.2 = bf16[2,3,1,384,1536]{4,3,2,1,0:T(8,128)(2,1)} collective-permute-done((bf16[2,3,1,384,1536]{4,3,2,1,0:T(8,128)(2,1)}, bf16[2,3,1,384,1536]{4,3,2,1,0:T(8,128)(2,1)}, u32[]{:S(2)}, u32[]{:S(2)}) %collective-permute-start.2) | collective-permute-done | bytes 7077920 | tf_op jit(solution)/shard_map/ppermute | solution.py:14
  231.5 9.9 %pad_maximum_fusion = bf16[2,3,3,384,1536]{4,3,2,1,0:T(8,128)(2,1)S(1)} fusion(bf16[2,3,1,384,1536]{4,3,2,1,0:T(8,128)(2,1)} %collective-permute-done.3, bf16[2,3,1,384,1536]{4,3,2,1,0:T(8,128)(2,1)} %constant_dynamic-update-slice_fusion.1, bf16[2,3,1,384,1536]{4,3,2,1,0:T(8,128)(2,1)} %collective-permute-done.2), kind=kLoop, calls=%fused_computation.55 | loop fusion | flops 21233664 | bytes 42467328 | tf_op jit(solution)/shard_map/concatenate | solution.py:18
  241.4 7.7 %fusion.44 = (bf16[1,3,3,384,1536]{4,3,2,1,0:T(8,128)(2,1)}, bf16[1,3,3,384,1536]{4,3,2,1,0:T(8,128)(2,1)}) fusion(bf16[2,3,3,384,1536]{4,3,2,1,0:T(8,128)(2,1)S(1)} %pad_maximum_fusion), kind=kLoop, calls=%fused_computation.69 | loop fusion | bytes 42467328 | tf_op jit(solution)/shard_map/slice | solution.py:75
  250.3 19.9 %concatenate.36 = bf16[3456,12,128]{2,1,0:T(8,128)(2,1)} reshape(bf16[9,384,1536]{2,1,0:T(8,128)(2,1)} %bitcast_dynamic-update-slice_fusion) | data formatting | bytes 21233664 | tf_op jit(solution)/shard_map/concatenate | solution.py:78
  270.2 17.8 %maximum_bitcast_fusion.1 = bf16[12,3712,128]{2,0,1:T(8,128)(2,1)S(1)} fusion(bf16[256,12,128]{2,1,0:T(8,128)(2,1)S(1)} %copy.23, bf16[3456,12,128]{2,1,0:T(8,128)(2,1)} %concatenate.36), kind=kLoop, calls=%fused_computation.57 | loop fusion | flops 5701632 | bytes 22806528 | tf_op jit(solution)/shard_map/transpose | solution.py:37
  288.0 5.7 %copy.26 = bf16[12,3712,128]{2,1,0:T(8,128)(2,1)} copy(bf16[12,3712,128]{2,0,1:T(8,128)(2,1)S(1)} %maximum_bitcast_fusion.1) | data formatting | bytes 22806528
  294.8 19.9 %concatenate.33 = bf16[3456,12,128]{2,1,0:T(8,128)(2,1)} reshape(bf16[9,384,1536]{2,1,0:T(8,128)(2,1)} %bitcast_dynamic-update-slice_fusion.1) | data formatting | bytes 21233664 | tf_op jit(solution)/shard_map/concatenate | solution.py:77
  314.7 17.8 %maximum_bitcast_fusion = bf16[12,3712,128]{2,0,1:T(8,128)(2,1)S(1)} fusion(bf16[256,12,128]{2,1,0:T(8,128)(2,1)S(1)} %copy.21, bf16[3456,12,128]{2,1,0:T(8,128)(2,1)} %concatenate.33), kind=kLoop, calls=%fused_computation.56 | loop fusion | flops 5701632 | bytes 22806528 | tf_op jit(solution)/shard_map/transpose | solution.py:36
  332.6 5.6 %copy.25 = bf16[12,3712,128]{2,1,0:T(8,128)(2,1)} copy(bf16[12,3712,128]{2,0,1:T(8,128)(2,1)S(1)} %maximum_bitcast_fusion) | data formatting | bytes 22806528
  338.2 174.0 %while.15 = (s32[]{:T(128)}, bf16[12,384,128]{1,2,0:T(8,128)(2,1)S(1)}, s32[12,2]{0,1:T(2,128)S(1)}, bf16[12,384,128]{1,2,0:T(8,128)(2,1)}, bf16[12,3712,128]{2,...) while((s32[]{:T(128)}, ...), condition=%wide.region_3.4_spmd.clone, body=%wide.region_0.3_spmd.clone.sunk | while | flops 743005184 | bytes 19647704 | solution.py:53
  338.2 4.5 select_reduce_fusion.2
  343.5 2.6 fusion.57
  346.7 2.5 fusion.58
  352.7 4.5 select_reduce_fusion.2
  358.0 2.6 fusion.57
  361.2 2.5 fusion.58
  364.8 2.2 fusion.60
  367.2 4.5 select_reduce_fusion.2
  372.5 2.6 fusion.57
  375.7 2.5 fusion.58
  379.3 2.2 fusion.60
  381.7 4.5 select_reduce_fusion.2
  387.0 2.6 fusion.57
  390.2 2.5 fusion.58
  393.8 2.2 fusion.60
  396.2 4.5 select_reduce_fusion.2
  401.5 2.6 fusion.57
  404.7 2.5 fusion.58
  408.3 2.2 fusion.60
  410.7 4.5 select_reduce_fusion.2
  416.0 2.6 fusion.57
  419.2 2.5 fusion.58
  422.8 2.2 fusion.60
  425.2 4.5 select_reduce_fusion.2
  430.5 2.6 fusion.57
  433.7 2.5 fusion.58
  437.3 2.2 fusion.60
  439.7 4.5 select_reduce_fusion.2
  445.0 2.6 fusion.57
  448.2 2.5 fusion.58
  451.8 2.2 fusion.60
  454.2 4.5 select_reduce_fusion.2
  459.5 2.6 fusion.57
  462.7 2.5 fusion.58
  466.3 2.2 fusion.60
  468.7 4.5 select_reduce_fusion.2
  474.0 2.6 fusion.57
  477.2 2.5 fusion.58
  480.8 2.2 fusion.60
  483.2 4.5 select_reduce_fusion.2
  488.5 2.6 fusion.57
  491.7 2.5 fusion.58
  495.3 2.2 fusion.60
  497.7 4.5 select_reduce_fusion.2
  503.0 2.6 fusion.57
  506.2 2.5 fusion.58
  509.8 2.2 fusion.60
  (144 shorter events, 53.1 us)
Async XLA Ops:
  6.5 56.3 %copy-start = (bf16[2,1,1,384,1536]{4,3,2,1,0:T(8,128)(2,1)S(1)}, bf16[2,1,1,384,1536]{4,3,2,1,0:T(8,128)(2,1)}, u32[]{:S(2)}) copy-start(bf16[2,1,1,384,1536]{4,3,2,1,0:T(8,128)(2,1)} %param.16) | copy-start | bytes 7077892
  6.5 161.7 %all-gather.2.cloned.1.call-start = ((), (), s32[]{:S(2)}) async-start(), calls=%async_computation | async-start | bytes 1671168 | tf_op jit(solution)/shard_map/all_gather | solution.py:87
  6.5 54.7 %collective-permute-start = (bf16[2,1,1,384,1536]{4,3,2,1,0:T(8,128)(2,1)}, bf16[2,1,1,384,1536]{4,3,2,1,0:T(8,128)(2,1)S(1)}, u32[]{:S(2)}, u32[]{:S(2)}) collective-permute-start(bf16[2,1,1,384,1536]{4,3,2,1,0:T(8,128)(2,1)} %param.16), channel_id=1, source_target_pairs={{0,16},{16,32},{32,48},{48,64},{64,80},{80,96},{96,112},{112,128},... | collective-permute-start | bytes 7077896 | tf_op jit(solution)/shard_map/ppermute | solution.py:14
  11.2 54.0 %collective-permute-start.1 = (bf16[2,1,1,384,1536]{4,3,2,1,0:T(8,128)(2,1)}, bf16[2,1,1,384,1536]{4,3,2,1,0:T(8,128)(2,1)S(1)}, u32[]{:S(2)}, u32[]{:S(2)}) collective-permute-start(bf16[2,1,1,384,1536]{4,3,2,1,0:T(8,128)(2,1)} %param.16), channel_id=1, source_target_pairs={{16,0},{32,16},{48,32},{64,48},{80,64},{96,80},{112,96},{128,112},... | collective-permute-start | bytes 7077896 | tf_op jit(solution)/shard_map/ppermute | solution.py:17
  62.8 11.9 %copy-start.5 = (bf16[2,16,1536]{2,1,0:T(8,128)(2,1)S(1)}, bf16[2,16,1536]{2,1,0:T(8,128)(2,1)}, u32[]{:S(2)}) copy-start(bf16[2,16,1536]{2,1,0:T(8,128)(2,1)} %param.17) | copy-start | bytes 294916
  62.8 12.9 %copy-start.1 = (bf16[1,1,384,1536]{3,2,1,0:T(8,128)(2,1)S(1)}, bf16[1,1,384,1536]{3,2,1,0:T(8,128)(2,1)}, u32[]{:S(2)}) copy-start(bf16[1,1,384,1536]{3,2,1,0:T(8,128)(2,1)} %param.13) | copy-start | bytes 3538948
  66.8 164.8 %collective-permute-start.2 = (bf16[2,3,1,384,1536]{4,3,2,1,0:T(8,128)(2,1)}, bf16[2,3,1,384,1536]{4,3,2,1,0:T(8,128)(2,1)}, u32[]{:S(2)}, u32[]{:S(2)}) collective-permute-start(bf16[2,3,1,384,1536]{4,3,2,1,0:T(8,128)(2,1)} %constant_dynamic-update-slice_fusion.1), channel_id=1, source_target_pairs={{0,1},{1,2},{2,3},{3,4},{4,5},{5,6},{6,7},{7,8},{8,9},{9,10},{10,1... | collective-permute-start | bytes 21233672 | tf_op jit(solution)/shard_map/ppermute | solution.py:14
  71.7 159.9 %collective-permute-start.3 = (bf16[2,3,1,384,1536]{4,3,2,1,0:T(8,128)(2,1)}, bf16[2,3,1,384,1536]{4,3,2,1,0:T(8,128)(2,1)}, u32[]{:S(2)}, u32[]{:S(2)}) collective-permute-start(bf16[2,3,1,384,1536]{4,3,2,1,0:T(8,128)(2,1)} %constant_dynamic-update-slice_fusion.1), channel_id=1, source_target_pairs={{1,0},{2,1},{3,2},{4,3},{5,4},{6,5},{7,6},{8,7},{9,8},{10,9},{11,1... | collective-permute-start | bytes 21233672 | tf_op jit(solution)/shard_map/ppermute | solution.py:17
  241.4 7.8 %copy-start.2 = (bf16[1,1,384,1536]{3,2,1,0:T(8,128)(2,1)S(1)}, bf16[1,1,384,1536]{3,2,1,0:T(8,128)(2,1)}, u32[]{:S(2)}) copy-start(bf16[1,1,384,1536]{3,2,1,0:T(8,128)(2,1)} %param.15) | copy-start | bytes 3538948
  288.0 5.7 %copy-start.3 = (bf16[1,1,384,1536]{3,2,1,0:T(8,128)(2,1)S(1)}, bf16[1,1,384,1536]{3,2,1,0:T(8,128)(2,1)}, u32[]{:S(2)}) copy-start(bf16[1,1,384,1536]{3,2,1,0:T(8,128)(2,1)} %param.14) | copy-start | bytes 3538948
  332.6 5.6 %copy-start.4 = (bf16[12,384,128]{1,2,0:T(8,128)(2,1)S(1)}, bf16[12,384,128]{1,2,0:T(8,128)(2,1)}, u32[]{:S(2)}) copy-start(bf16[12,384,128]{1,2,0:T(8,128)(2,1)} %custom-call.1) | copy-start | bytes 3538948
  332.6 5.6 %copy-start.6 = (s32[12,2]{0,1:T(2,128)S(1)}, s32[12,2]{0,1:T(2,128)}, u32[]{:S(2)}) copy-start(s32[12,2]{0,1:T(2,128)} %param.18) | copy-start | bytes 292
Sparse Core Ops, SparseCore 0:
  75.6 92.5 all-gather.1
where the time goes:
time: 528 us; the launch traced here: 520 us
  waiting for transfers between devices  192 us (36%)
  other arithmetic  155 us (29%)
  local copies, waits for them, and re-layouts  90.6 us (17%)
  matrix products  55.5 us (11%)
  starting transfers between devices  13.9 us (3%)
  between operations  13.6 us (3%)
    ppermute x2, waiting for transfers between devices, extended(): lax.ppermute(lax.slice_in_dim(block, block.shape[dim] - width, None, axis...  101 us
    all_gather x1, waiting for transfers between devices, on_device(): text_both = lax.all_gather(text_kv, 'space', axis=1, tiled=True)  90.4 us
    gather x36, other arithmetic, attend_tile(): tile_valid = slot_valid[tile_of]  56.3 us
    and x12, other arithmetic, one_head(): tile_valid & (jnp.abs(step_time) <= reach[0])  30.8 us
    dot_general x12, matrix products, one_head(): jnp.dot(query_head, key_head.T, preferred_element_type=jnp.float32) * scale  29.6 us
    dot_general x12, matrix products, one_head(): jnp.dot(weights.astype(jnp.bfloat16), value_head, preferred_element_type=...  25.8 us
    concatenate x2, local copies, waits for them, and re-layouts, tile_output(): value_rows = jnp.concatenate([near_values, text_both[1]], axis=0)  21.8 us
    concatenate x2, local copies, waits for them, and re-layouts, tile_output(): key_rows = jnp.concatenate([near_keys, text_both[0]], axis=0)  20.9 us
  transfers between devices with their start and end apart: 5, of which 4 were waited for; matrix products, arithmetic and copies ran while one was open for 3% of the time, Pallas kernels for 0%

commit v1 on v0

v1 whole, which is shorter than its diff:
```python
import math

import jax
import jax.numpy as jnp
from jax import lax
from jax.experimental import pallas as pl
from jax.experimental.pallas import tpu as pltpu
from jax.sharding import PartitionSpec as P

MESH = pl.DeviceIdType.MESH
HEAD = 128
GROUP = 3
HEADS = 12
LANES = 128
ROW_BLOCK = 384


def kernel(
    query, fresh_key, fresh_value, stale, text, window, text_len, out,
    q_all, k_all, v_all, stale_all, words, out_all,
    pack11, pack10, pack01, packq,
    got11, got10, got01, gotq,
    o_send, o_stat, o_got, o_got_stat,
    peak, total, mixed, done, order, place,
    load_sem, send_sem, recv_sem, text_send, text_recv,
):
    rows = q_all.shape[1]
    times = lax.axis_size("tm")
    spaces = lax.axis_size("space")
    time = lax.axis_index("tm")
    space = lax.axis_index("space")
    core = lax.rem(space, 2)
    low = lax.rem(space // 2, 2)
    column = space // 4
    has_time = (time > 0, time < times - 1)
    has_space = (space > 0, space < spaces - 1)
    next_time = (time - 1, time + 1)
    next_space = (space - 1, space + 1)
    scale = math.log2(math.e) / math.sqrt(HEAD)

    mine = words.at[core, column, low]
    for head in range(HEADS):
        at = pl.ds(head * HEAD, HEAD)
        pltpu.make_async_copy(stale.at[:, :, at], stale_all.at[head], load_sem.at[0]).start()
    for head in range(HEADS):
        at = pl.ds(head * HEAD, HEAD)
        pltpu.make_async_copy(query.at[:, at], q_all.at[head], load_sem.at[1]).start()
        pltpu.make_async_copy(text.at[:, :, at], mine.at[head], load_sem.at[2]).start()
    for head in range(HEADS):
        at = pl.ds(head * HEAD, HEAD)
        pltpu.make_async_copy(fresh_key.at[:, at], k_all.at[head], load_sem.at[3]).start()
        pltpu.make_async_copy(fresh_value.at[:, at], v_all.at[head], load_sem.at[4]).start()
    loads = [
        pltpu.make_async_copy(target, target, load_sem.at[i])
        for i, target in enumerate((stale_all, q_all, mine, k_all, v_all))
    ]

    partner_low = column * 4 + (1 - low) * 2 + core
    sibling = space + 1 - 2 * core
    barrier = pltpu.get_barrier_semaphore()
    partners = [
        {"tm": lax.rem(time + 1, times)},
        {"tm": lax.rem(time + times - 1, times)},
        {"space": lax.rem(space + 1, spaces)},
        {"space": lax.rem(space + spaces - 1, spaces)},
        {"space": partner_low},
    ] + [{"space": lax.rem(space + 4 * d, spaces)} for d in (1, 2, 3)]
    for partner in partners:
        pl.semaphore_signal(barrier, inc=1, device_id=partner, device_id_type=MESH)

    counts = [jnp.int32(0)] * 4
    slots = []
    for head in range(HEADS):
        reach_time, reach_space = window[head, 0], window[head, 1]
        both = reach_time * reach_space
        hits = [both, reach_time - both, reach_space - both, 1 - reach_time - reach_space + both]
        slot = jnp.int32(0)
        for k in range(4):
            slot = slot + hits[k] * (GROUP * k + counts[k])
            counts[k] = counts[k] + hits[k]
        slots.append(slot)
        place[head] = jnp.minimum(slot, HEADS - 1)
    for s in range(HEADS):
        chosen = jnp.int32(0)
        for head in range(HEADS):
            apart = jnp.maximum(slots[head] - s, s - slots[head])
            chosen = chosen + head * jnp.maximum(1 - apart, 0)
        order[s] = chosen

    def pack(target, base):
        for g in range(GROUP):
            target[:, g] = stale_all[order[base + g]]

    def along_time(kind, d, source, target):
        return pltpu.make_async_remote_copy(
            src_ref=source, dst_ref=target.at[1 - d],
            send_sem=send_sem.at[kind, d], recv_sem=recv_sem.at[kind, 1 - d],
            device_id={"tm": time - 1 + 2 * d}, device_id_type=MESH,
        )

    def along_space(kind, d, source, target):
        return pltpu.make_async_remote_copy(
            src_ref=source, dst_ref=target.at[1 - d],
            send_sem=send_sem.at[kind, d], recv_sem=recv_sem.at[kind, 1 - d],
            device_id={"space": space - 1 + 2 * d}, device_id_type=MESH,
        )

    def send_both(has, make, kind, source, target):
        for d in (0, 1):
            @pl.when(has[d])
            def _():
                make(kind, d, source, target).start()

    def arrived(has, make, kind, source, target):
        for d in (0, 1):
            @pl.when(has[d])
            def _():
                make(kind, 1 - d, source, target).wait_recv()

    def sent(has, make, kind, source, target):
        for d in (0, 1):
            @pl.when(has[d])
            def _():
                make(kind, d, source, target).wait_send()

    loads[0].wait()
    pack(pack11, 0)
    pl.semaphore_wait(barrier, len(partners))
    send_both(has_time, along_time, 0, pack11, got11)
    loads[1].wait()
    for g in range(GROUP):
        packq[g] = q_all[order[g]]
    send_both(has_space, along_space, 3, packq, gotq)
    loads[2].wait()
    swap = pltpu.make_async_remote_copy(
        src_ref=mine, dst_ref=mine, send_sem=text_send.at[0], recv_sem=text_recv.at[0],
        device_id={"space": partner_low}, device_id_type=MESH,
    )
    swap.start()
    pack(pack01, 2 * GROUP)
    send_both(has_space, along_space, 2, pack01, got01)
    pack(pack10, GROUP)
    send_both(has_time, along_time, 1, pack10, got10)

    swap.wait_recv()
    pair = words.at[core, column]
    spread = [
        pltpu.make_async_remote_copy(
            src_ref=pair, dst_ref=pair, send_sem=text_send.at[d], recv_sem=text_recv.at[d],
            device_id={"space": lax.rem(space + 4 * d, spaces)}, device_id_type=MESH,
        )
        for d in (1, 2, 3)
    ]
    for copy in spread:
        copy.start()

    def attend(state, query_rows, keys, values, first=False, live=None):
        ones = jnp.ones((keys.shape[0], LANES), jnp.bfloat16)
        values = jnp.concatenate([values, ones], axis=1)
        parts = keys.shape[0] // LANES
        for at in range(0, rows, ROW_BLOCK):
            here = pl.ds(at, ROW_BLOCK)
            scores = lax.dot_general(
                query_rows[at : at + ROW_BLOCK], keys, (((1,), (1,)), ((), ())),
                preferred_element_type=jnp.float32,
            ) * scale
            if live is not None:
                scores = jnp.where(live, scores, -1e30)
            top = jnp.broadcast_to(jnp.max(scores, axis=1, keepdims=True), (ROW_BLOCK, LANES))
            if not first:
                before = peak[state, here]
                top = jnp.maximum(before, top)
            weights = jnp.exp2(scores - jnp.concatenate([top] * parts, axis=1)).astype(jnp.bfloat16)
            both = jnp.dot(weights, values, preferred_element_type=jnp.float32)
            peak[state, here] = top
            if first:
                mixed[state, here] = both[:, :HEAD]
                total[state, here] = both[:, HEAD:]
            else:
                shrink = jnp.exp2(before - top)
                mixed[state, here] = mixed[state, here] * shrink + both[:, :HEAD]
                total[state, here] = total[state, here] * shrink + both[:, HEAD:]

    def own_query(slot):
        return q_all[order[slot]]

    loads[3].wait()
    loads[4].wait()

    @pl.loop(0, HEADS)
    def _(slot):
        head = order[slot]
        attend(slot, q_all[head], k_all[head], v_all[head], first=True)

    arrived(has_space, along_space, 3, packq, gotq)

    def side_ok(d, position, count):
        return jnp.where(d == 0, position > 0, position < count - 1)

    @pl.loop(0, 2)
    def _(d):
        @pl.when(side_ok(d, space, spaces))
        def _():
            @pl.loop(0, GROUP)
            def _(g):
                attend(HEADS + d * GROUP + g, gotq[d, g], pack11[0, g], pack11[1, g], first=True)

    for copy in spread:
        copy.wait_recv()
    half = words.at[core]
    across = pltpu.make_async_remote_copy(
        src_ref=half, dst_ref=half, send_sem=text_send.at[4], recv_sem=text_recv.at[4],
        device_id={"space": sibling}, device_id_type=MESH,
    )
    across.start()
    across.wait_recv()
    count = 2 * spaces // 2 * words.shape[5]
    index = lax.broadcasted_iota(jnp.int32, (1, count), 1)
    token = (((index // 32) % 4) * 4 + ((index // 16) % 2) * 2 + index // 128) * 16 + index % 16
    live = token < text_len[0]

    @pl.loop(0, HEADS)
    def _(slot):
        head = order[slot]
        keys = words[:, :, :, head, 0].reshape(count, HEAD)
        values = words[:, :, :, head, 1].reshape(count, HEAD)
        attend(slot, q_all[head], keys, values, live=live)

    arrived(has_time, along_time, 0, pack11, got11)
    lane = lax.broadcasted_iota(jnp.int32, (rows, LANES), 1)

    @pl.loop(0, 2)
    def _(i):
        d = lax.rem(i + core, 2)

        @pl.when(side_ok(d, space, spaces))
        def _():
            @pl.loop(0, GROUP)
            def _(g):
                state = HEADS + d * GROUP + g

                @pl.loop(0, 2)
                def _(e):
                    @pl.when(side_ok(e, time, times))
                    def _():
                        attend(state, gotq[d, g], got11[e, 0, g], got11[e, 1, g])

                o_send[d, g] = (mixed[state] / total[state]).astype(jnp.bfloat16)

            stats = jnp.zeros((rows, LANES), jnp.float32)
            for g in range(GROUP):
                state = HEADS + d * GROUP + g
                stats = jnp.where(lane == g, peak[state] + jnp.log2(total[state]), stats)
            o_stat[d] = stats.T[:8]
            along_space(4, d, o_send.at[d], o_got).start()
            along_space(5, d, o_stat.at[d], o_got_stat).start()

    @pl.loop(0, 2)
    def _(e):
        @pl.when(side_ok(e, time, times))
        def _():
            @pl.loop(0, GROUP)
            def _(g):
                attend(g, own_query(g), got11[e, 0, g], got11[e, 1, g])

    arrived(has_space, along_space, 2, pack01, got01)

    @pl.loop(0, 2)
    def _(e):
        @pl.when(side_ok(e, space, spaces))
        def _():
            @pl.loop(0, GROUP)
            def _(g):
                attend(2 * GROUP + g, own_query(2 * GROUP + g), got01[e, 0, g], got01[e, 1, g])

    arrived(has_time, along_time, 1, pack10, got10)

    @pl.loop(0, 2)
    def _(e):
        @pl.when(side_ok(e, time, times))
        def _():
            @pl.loop(0, GROUP)
            def _(g):
                attend(GROUP + g, own_query(GROUP + g), got10[e, 0, g], got10[e, 1, g])

    @pl.loop(GROUP, HEADS)
    def _(slot):
        done[slot] = (mixed[slot] / total[slot]).astype(jnp.bfloat16)

    for d in (0, 1):
        @pl.when(has_space[d])
        def _():
            along_space(4, 1 - d, o_send.at[1 - d], o_got).wait_recv()
            along_space(5, 1 - d, o_stat.at[1 - d], o_got_stat).wait_recv()
            spare = jnp.zeros((LANES - 8, rows), jnp.float32)
            stats = jnp.concatenate([o_got_stat[d], spare], axis=0).T
            for g in range(GROUP):
                other = jnp.broadcast_to(stats[:, g : g + 1], (rows, LANES))
                before = peak[g]
                top = jnp.maximum(before, other)
                keep = jnp.exp2(before - top)
                add = jnp.exp2(other - top)
                peak[g] = top
                mixed[g] = mixed[g] * keep + o_got[d, g].astype(jnp.float32) * add
                total[g] = total[g] * keep + add

    for g in range(GROUP):
        done[g] = (mixed[g] / total[g]).astype(jnp.bfloat16)
    for head in range(HEADS):
        out_all[:, head * HEAD : (head + 1) * HEAD] = done[place[head]]
    store = pltpu.make_async_copy(out_all, out, load_sem.at[5])
    store.start()

    sent(has_time, along_time, 0, pack11, got11)
    sent(has_time, along_time, 1, pack10, got10)
    sent(has_space, along_space, 2, pack01, got01)
    sent(has_space, along_space, 3, packq, gotq)
    for d in (0, 1):
        @pl.when(has_space[d])
        def _():
            along_space(4, d, o_send.at[d], o_got).wait_send()
            along_space(5, d, o_stat.at[d], o_got_stat).wait_send()
    swap.wait_send()
    for copy in spread:
        copy.wait_send()
    across.wait_send()
    store.wait()


def on_device(query, fresh_key, fresh_value, stale_kv, text_kv, window, text_len):
    rows, width = query.shape[2:]
    words = text_kv.shape[1]
    bf16, f32 = jnp.bfloat16, jnp.float32
    heads = (GROUP, rows, HEAD)
    anywhere = pl.BlockSpec(memory_space=pl.ANY)
    scalars = pl.BlockSpec(memory_space=pltpu.SMEM)
    result = pl.pallas_call(
        kernel,
        out_shape=jax.ShapeDtypeStruct((rows, width), bf16),
        in_specs=[anywhere] * 5 + [scalars] * 2,
        out_specs=anywhere,
        scratch_shapes=[
            pltpu.VMEM((HEADS, rows, HEAD), bf16),
            pltpu.VMEM((HEADS, rows, HEAD), bf16),
            pltpu.VMEM((HEADS, rows, HEAD), bf16),
            pltpu.VMEM((HEADS, 2, rows, HEAD), bf16),
            pltpu.VMEM((2, 4, 2, HEADS, 2, words, HEAD), bf16),
            pltpu.VMEM((rows, width), bf16),
            pltpu.VMEM((2, *heads), bf16),
            pltpu.VMEM((2, *heads), bf16),
            pltpu.VMEM((2, *heads), bf16),
            pltpu.VMEM(heads, bf16),
            pltpu.VMEM((2, 2, *heads), bf16),
            pltpu.VMEM((2, 2, *heads), bf16),
            pltpu.VMEM((2, 2, *heads), bf16),
            pltpu.VMEM((2, *heads), bf16),
            pltpu.VMEM((2, *heads), bf16),
            pltpu.VMEM((2, 8, rows), f32),
            pltpu.VMEM((2, *heads), bf16),
            pltpu.VMEM((2, 8, rows), f32),
            pltpu.VMEM((HEADS + 2 * GROUP, rows, LANES), f32),
            pltpu.VMEM((HEADS + 2 * GROUP, rows, LANES), f32),
            pltpu.VMEM((HEADS + 2 * GROUP, rows, HEAD), f32),
            pltpu.VMEM((HEADS, rows, HEAD), bf16),
            pltpu.SMEM((HEADS,), jnp.int32),
            pltpu.SMEM((HEADS,), jnp.int32),
            pltpu.SemaphoreType.DMA((6,)),
            pltpu.SemaphoreType.DMA((6, 2)),
            pltpu.SemaphoreType.DMA((6, 2)),
            pltpu.SemaphoreType.DMA((5,)),
            pltpu.SemaphoreType.DMA((5,)),
        ],
        compiler_params=pltpu.CompilerParams(
            collective_id=0, has_side_effects=True, vmem_limit_bytes=50 << 20
        ),
    )(
        query[0, 0], fresh_key[0, 0], fresh_value[0, 0], stale_kv[:, 0, 0], text_kv,
        window, text_len,
    )
    return result[None, None]


def solution(mesh):
    in_specs = (
        P("tm", "space", None, None),
        P("tm", "space", None, None),
        P("tm", "space", None, None),
        P(None, "tm", "space", None, None),
        P(None, "space", None),
        P(),
        P(),
    )
    out_specs = P("tm", "space", None, None)
    return jax.shard_map(
        on_device, mesh=mesh, in_specs=in_specs, out_specs=out_specs, check_vma=False
    )
```

time: 528 us -> 88.4 us (0.17); the launches traced: 520 us -> 87.2 us
  waiting for transfers between devices: 192 us -> 0 us
  other arithmetic: 155 us -> 0 us
  local copies, waits for them, and re-layouts: 90.6 us -> 5.22 us
  Pallas kernels: 0 us -> 81.3 us
  matrix products: 55.5 us -> 0 us
  starting transfers between devices: 13.9 us -> 0 us
  between operations: 13.6 us -> 0.66 us
    ppermute x4 -> x0, waiting for transfers between devices: 101 us -> none  [the longest x2 101 us: extended(): lax.ppermute(lax.slice_in_dim(block, block.shape[dim] - width, None, axis...]
    all_gather x1 -> x0, waiting for transfers between devices: 90.4 us -> none  [on_device(): text_both = lax.all_gather(text_kv, 'space', axis=1, tiled=True)]
    pallas_call x0 -> x1, Pallas kernels: none -> 81.3 us  [on_device(): pl.pallas_call(kernel, out_shape=jax.ShapeDtypeStruct((rows, width), bf16...]
    gather x36 -> x0, other arithmetic: 56.3 us -> none  [attend_tile(): tile_valid = slot_valid[tile_of]]
    dot_general x24 -> x0, matrix products: 55.5 us -> none  [the longest x12 29.6 us: one_head(): jnp.dot(query_head, key_head.T, preferred_element_type=jnp.float32) * scale]
    concatenate x5 -> x0, local copies, waits for them, and re-layouts: 44.3 us -> none  [the longest x2 21.8 us: tile_output(): value_rows = jnp.concatenate([near_values, text_both[1]], axis=0)]
    transpose x2 -> x0, other arithmetic: 35.7 us -> none  [the longest x1 17.8 us: attend_tile(): key_heads = key_rows.reshape(-1, heads, head_dim).transpose(1, 0, 2)]
    and x14 -> x0, other arithmetic: 30.9 us -> none  [the longest x12 30.8 us: one_head(): tile_valid & (jnp.abs(step_time) <= reach[0])]
  transfers between devices with their start and end apart: 5 -> 0, of which waited for: 4 -> 0; matrix products, arithmetic and copies ran while one was open for 3% -> 0% of each run, Pallas kernels for 0% -> 0%
where the time goes in v1:
time: 88.4 us; the launch traced here: 87.2 us
  Pallas kernels  81.3 us (92%)
  local copies, waits for them, and re-layouts  5.22 us (6%)
    pallas_call x1, Pallas kernels, on_device(): pl.pallas_call(kernel, out_shape=jax.ShapeDtypeStruct((rows, width), bf16...  81.3 us
    unnamed x8, local copies, waits for them, and re-layouts  5.22 us

profile of v1, /device:TPU:1, one launch (start us, length us, event | category | flops | bytes accessed | tf_op | source)
XLA Modules:
  0.0 87.2 jit_solution(5780867902198377961)
XLA Ops:
  0.7 0.8 copy.8.window
  1.4 0.0 copy-start
  1.4 1.3 %copy-done = bf16[1,1,384,1536]{3,2,1,0:T(8,128)(2,1)S(1)} copy-done((bf16[1,1,384,1536]{3,2,1,0:T(8,128)(2,1)S(1)}, bf16[1,1,384,1536]{3,2,1,0:T(8,128)(2,1)}, u32[]{:S(2)}) %copy-start) | copy-done | bytes 1179672
  2.7 0.0 copy-start.1
  2.7 1.3 %copy-done.1 = bf16[1,1,384,1536]{3,2,1,0:T(8,128)(2,1)S(1)} copy-done((bf16[1,1,384,1536]{3,2,1,0:T(8,128)(2,1)S(1)}, bf16[1,1,384,1536]{3,2,1,0:T(8,128)(2,1)}, u32[]{:S(2)}) %copy-start.1) | copy-done | bytes 1179672
  4.0 0.0 copy-start.2
  4.0 0.9 %copy-done.2 = bf16[2,16,1536]{2,1,0:T(8,128)(2,1)S(1)} copy-done((bf16[2,16,1536]{2,1,0:T(8,128)(2,1)S(1)}, bf16[2,16,1536]{2,1,0:T(8,128)(2,1)}, u32[]{:S(2)}) %copy-start.2) | copy-done | bytes 98328
  4.9 81.3 %shard_map.73 = bf16[384,1536]{1,0:T(8,128)(2,1)S(1)} custom-call(bf16[384,1536]{1,0:T(8,128)(2,1)S(1)} %bitcast.6, bf16[384,1536]{1,0:T(8,128)(2,1)S(1)} %bitcast.7, bf16[384,1536]{1,0:T(8,128)(2,1)} %bitcast.9, bf16[2,384,1536]{2,1,0:T(8,128)(2,1)} %bitcast.8, bf16[2,16,1536]{2,1,0:T(8,128)(2,1)S(1)} %copy-done.2, s32[12,2]{1,0:T(8,128)S(1)} %copy.8.window, ...), custom_call_target="tpu_custom_call" | custom-call | tf_op jit(solution)/shard_map/pallas_call | solution.py:337
  86.2 1.0 %copy.11 = bf16[1,1,384,1536]{3,2,1,0:T(8,128)(2,1)} copy(bf16[1,1,384,1536]{3,2,1,0:T(8,128)(2,1)S(1)} %bitcast.5) | data formatting | bytes 2359296
Async XLA Ops:
  1.4 1.3 %copy-start = (bf16[1,1,384,1536]{3,2,1,0:T(8,128)(2,1)S(1)}, bf16[1,1,384,1536]{3,2,1,0:T(8,128)(2,1)}, u32[]{:S(2)}) copy-start(bf16[1,1,384,1536]{3,2,1,0:T(8,128)(2,1)} %param.7) | copy-start | bytes 3538948
  2.7 1.3 %copy-start.1 = (bf16[1,1,384,1536]{3,2,1,0:T(8,128)(2,1)S(1)}, bf16[1,1,384,1536]{3,2,1,0:T(8,128)(2,1)}, u32[]{:S(2)}) copy-start(bf16[1,1,384,1536]{3,2,1,0:T(8,128)(2,1)} %param.8) | copy-start | bytes 3538948
  4.0 0.9 %copy-start.2 = (bf16[2,16,1536]{2,1,0:T(8,128)(2,1)S(1)}, bf16[2,16,1536]{2,1,0:T(8,128)(2,1)}, u32[]{:S(2)}) copy-start(bf16[2,16,1536]{2,1,0:T(8,128)(2,1)} %text.1) | copy-start | bytes 294916

commit v2 on v1

--- a/solution.py
+++ b/solution.py
@@ -1,3 +1,4 @@
+import functools
 import math
 
 import jax
@@ -154,56 +155,137 @@
     for copy in spread:
         copy.start()
 
-    def attend(state, query_rows, keys, values, first=False, live=None):
-        ones = jnp.ones((keys.shape[0], LANES), jnp.bfloat16)
-        values = jnp.concatenate([values, ones], axis=1)
-        parts = keys.shape[0] // LANES
-        for at in range(0, rows, ROW_BLOCK):
-            here = pl.ds(at, ROW_BLOCK)
-            scores = lax.dot_general(
-                query_rows[at : at + ROW_BLOCK], keys, (((1,), (1,)), ((), ())),
+    def rows_at(block):
+        return pl.ds(block * ROW_BLOCK, ROW_BLOCK)
+
+    def attend(jobs):
+        for job in jobs:
+            job["keys"] = jnp.concatenate([chunk[0] for chunk in job["chunks"]], axis=0)
+            values = jnp.concatenate([chunk[1] for chunk in job["chunks"]], axis=0)
+            ones = jnp.ones((values.shape[0], LANES), jnp.bfloat16)
+            job["values"] = jnp.concatenate([values, ones], axis=1)
+        tasks = [dict(job, here=rows_at(block)) for job in jobs for block in range(rows // ROW_BLOCK)]
+
+        def score(task):
+            query_rows = task["query"](task["here"])
+            task["scores"] = lax.dot_general(
+                query_rows, task["keys"], (((1,), (1,)), ((), ())),
                 preferred_element_type=jnp.float32,
             ) * scale
-            if live is not None:
-                scores = jnp.where(live, scores, -1e30)
-            top = jnp.broadcast_to(jnp.max(scores, axis=1, keepdims=True), (ROW_BLOCK, LANES))
-            if not first:
-                before = peak[state, here]
-                top = jnp.maximum(before, top)
-            weights = jnp.exp2(scores - jnp.concatenate([top] * parts, axis=1)).astype(jnp.bfloat16)
-            both = jnp.dot(weights, values, preferred_element_type=jnp.float32)
-            peak[state, here] = top
-            if first:
-                mixed[state, here] = both[:, :HEAD]
-                total[state, here] = both[:, HEAD:]
-            else:
-                shrink = jnp.exp2(before - top)
-                mixed[state, here] = mixed[state, here] * shrink + both[:, :HEAD]
-                total[state, here] = total[state, here] * shrink + both[:, HEAD:]
-
-    def own_query(slot):
-        return q_all[order[slot]]
+
+        def weigh(task):
+            pieces, tops, at = [], [], 0
+            before = task["before"](task["here"]) if task["before"] else None
+            for keys, _, live, valid in task["chunks"]:
+                piece = task["scores"][:, at : at + keys.shape[0]]
+                at += keys.shape[0]
+                if live is not None:
+                    piece = jnp.where(live, piece, -1e30)
+                top = jnp.broadcast_to(jnp.max(piece, axis=1, keepdims=True), (ROW_BLOCK, LANES))
+                if valid is not None:
+                    top = jnp.where(valid, top, -1e30)
+                pieces.append(piece)
+                tops.append(top)
+            top = functools.reduce(jnp.maximum, tops + ([before[0]] if before else []))
+            weights = []
+            for piece, (_, _, _, valid) in zip(pieces, task["chunks"]):
+                base = top if valid is None else jnp.where(valid, top, 1e30)
+                base = jnp.concatenate([base] * (piece.shape[1] // LANES), axis=1)
+                weights.append(jnp.exp2(piece - base).astype(jnp.bfloat16))
+            both = jnp.dot(
+                jnp.concatenate(weights, axis=1), task["values"], preferred_element_type=jnp.float32
+            )
+            mixed, total = both[:, :HEAD], both[:, HEAD:]
+            if before:
+                shrink = jnp.exp2(before[0] - top)
+                total = before[1] * shrink + total
+                mixed = before[2] * shrink + mixed
+            task["after"](task["here"], top, total, mixed)
+
+        score(tasks[0])
+        for i, task in enumerate(tasks):
+            if i + 1 < len(tasks):
+                score(tasks[i + 1])
+            weigh(task)
+
+    def job(query, chunks, after, before=None):
+        return {"query": query, "chunks": chunks, "before": before, "after": after}
+
+    def own(slot):
+        head = order[slot]
+        return lambda here: q_all[head, here]
+
+    def saved(g, state):
+        return lambda here: (peak[g][state, here], total[g][state, here], mixed[g][state, here])
+
+    def save(g, state):
+        def after(here, top, weight, value):
+            peak[g][state, here] = top
+            total[g][state, here] = weight
+            mixed[g][state, here] = value
+
+        return after
+
+    def finish(target, at):
+        def after(here, top, weight, value):
+            target[(*at, here)] = (value / weight).astype(jnp.bfloat16)
+
+        return after
+
+    def fresh(slot):
+        head = order[slot]
+        return k_all[head], v_all[head], None, None
+
+    def spoken(slot):
+        head = order[slot]
+        keys = words[:, :, :, head, 0].reshape(count, HEAD)
+        values = words[:, :, :, head, 1].reshape(count, HEAD)
+        return keys, values, live, None
+
+    def near(got, g, has):
+        return [(got[e, 0, g], got[e, 1, g], None, has[e]) for e in (0, 1)]
+
+    def side_ok(d, position, count):
+        return jnp.where(d == 0, position > 0, position < count - 1)
+
+    count = 2 * spaces // 2 * words.shape[5]
+    index = lax.broadcasted_iota(jnp.int32, (1, count), 1)
+    token = (((index // 32) % 4) * 4 + ((index // 16) % 2) * 2 + index // 128) * 16 + index % 16
+    live = token < text_len[0]
+
+    for d in (0, 1):
+        @pl.when(jnp.logical_not(has_time[d]))
+        def _():
+            got11[d] = jnp.zeros_like(got11[d])
+            got10[d] = jnp.zeros_like(got10[d])
+
+        @pl.when(jnp.logical_not(has_space[d]))
+        def _():
+            got01[d] = jnp.zeros_like(got01[d])
 
     loads[3].wait()
     loads[4].wait()
 
-    @pl.loop(0, HEADS)
-    def _(slot):
-        head = order[slot]
-        attend(slot, q_all[head], k_all[head], v_all[head], first=True)
+    @pl.loop(0, 3)
+    def _(kind):
+        attend([
+            job(own(kind * GROUP + g), [fresh(kind * GROUP + g)], save(g, kind))
+            for g in range(GROUP)
+        ])
 
     arrived(has_space, along_space, 3, packq, gotq)
 
-    def side_ok(d, position, count):
-        return jnp.where(d == 0, position > 0, position < count - 1)
+    def visitor(d, g):
+        return lambda here: gotq[d, g, here]
 
     @pl.loop(0, 2)
     def _(d):
         @pl.when(side_ok(d, space, spaces))
         def _():
-            @pl.loop(0, GROUP)
-            def _(g):
-                attend(HEADS + d * GROUP + g, gotq[d, g], pack11[0, g], pack11[1, g], first=True)
+            attend([
+                job(visitor(d, g), [(pack11[0, g], pack11[1, g], None, None)], save(g, 3 + d))
+                for g in range(GROUP)
+            ])
 
     for copy in spread:
         copy.wait_recv()
@@ -214,17 +296,10 @@
     )
     across.start()
     across.wait_recv()
-    count = 2 * spaces // 2 * words.shape[5]
-    index = lax.broadcasted_iota(jnp.int32, (1, count), 1)
-    token = (((index // 32) % 4) * 4 + ((index // 16) % 2) * 2 + index // 128) * 16 + index % 16
-    live = token < text_len[0]
-
-    @pl.loop(0, HEADS)
-    def _(slot):
-        head = order[slot]
-        keys = words[:, :, :, head, 0].reshape(count, HEAD)
-        values = words[:, :, :, head, 1].reshape(count, HEAD)
-        attend(slot, q_all[head], keys, values, live=live)
+    attend([
+        job(own(3 * GROUP + g), [fresh(3 * GROUP + g), spoken(3 * GROUP + g)], finish(done, (3 * GROUP + g,)))
+        for g in range(GROUP)
+    ])
 
     arrived(has_time, along_time, 0, pack11, got11)
     lane = lax.broadcasted_iota(jnp.int32, (rows, LANES), 1)
@@ -235,57 +310,38 @@
 
         @pl.when(side_ok(d, space, spaces))
         def _():
-            @pl.loop(0, GROUP)
-            def _(g):
-                state = HEADS + d * GROUP + g
-
-                @pl.loop(0, 2)
-                def _(e):
-                    @pl.when(side_ok(e, time, times))
-                    def _():
-                        attend(state, gotq[d, g], got11[e, 0, g], got11[e, 1, g])
-
-                o_send[d, g] = (mixed[state] / total[state]).astype(jnp.bfloat16)
-
+            def give(g):
+                def after(here, top, weight, value):
+                    o_send[d, g, here] = (value / weight).astype(jnp.bfloat16)
+                    peak[g][3 + d, here] = top + jnp.log2(weight)
+
+                return after
+
+            attend([
+                job(visitor(d, g), near(got11, g, has_time), give(g), saved(g, 3 + d))
+                for g in range(GROUP)
+            ])
             stats = jnp.zeros((rows, LANES), jnp.float32)
             for g in range(GROUP):
-                state = HEADS + d * GROUP + g
-                stats = jnp.where(lane == g, peak[state] + jnp.log2(total[state]), stats)
+                stats = jnp.where(lane == g, peak[g][3 + d], stats)
             o_stat[d] = stats.T[:8]
             along_space(4, d, o_send.at[d], o_got).start()
             along_space(5, d, o_stat.at[d], o_got_stat).start()
 
-    @pl.loop(0, 2)
-    def _(e):
-        @pl.when(side_ok(e, time, times))
-        def _():
-            @pl.loop(0, GROUP)
-            def _(g):
-                attend(g, own_query(g), got11[e, 0, g], got11[e, 1, g])
-
+    attend([
+        job(own(g), [spoken(g), *near(got11, g, has_time)], save(g, 0), saved(g, 0))
+        for g in range(GROUP)
+    ])
     arrived(has_space, along_space, 2, pack01, got01)
-
-    @pl.loop(0, 2)
-    def _(e):
-        @pl.when(side_ok(e, space, spaces))
-        def _():
-            @pl.loop(0, GROUP)
-            def _(g):
-                attend(2 * GROUP + g, own_query(2 * GROUP + g), got01[e, 0, g], got01[e, 1, g])
-
+    attend([
+        job(own(2 * GROUP + g), [spoken(2 * GROUP + g), *near(got01, g, has_space)], finish(done, (2 * GROUP + g,)), saved(g, 2))
+        for g in range(GROUP)
+    ])
     arrived(has_time, along_time, 1, pack10, got10)
-
-    @pl.loop(0, 2)
-    def _(e):
-        @pl.when(side_ok(e, time, times))
-        def _():
-            @pl.loop(0, GROUP)
-            def _(g):
-                attend(GROUP + g, own_query(GROUP + g), got10[e, 0, g], got10[e, 1, g])
-
-    @pl.loop(GROUP, HEADS)
-    def _(slot):
-        done[slot] = (mixed[slot] / total[slot]).astype(jnp.bfloat16)
+    attend([
+        job(own(GROUP + g), [spoken(GROUP + g), *near(got10, g, has_time)], finish(done, (GROUP + g,)), saved(g, 1))
+        for g in range(GROUP)
+    ])
 
     for d in (0, 1):
         @pl.when(has_space[d])
@@ -296,16 +352,16 @@
             stats = jnp.concatenate([o_got_stat[d], spare], axis=0).T
             for g in range(GROUP):
                 other = jnp.broadcast_to(stats[:, g : g + 1], (rows, LANES))
-                before = peak[g]
+                before = peak[g][0]
                 top = jnp.maximum(before, other)
                 keep = jnp.exp2(before - top)
                 add = jnp.exp2(other - top)
-                peak[g] = top
-                mixed[g] = mixed[g] * keep + o_got[d, g].astype(jnp.float32) * add
-                total[g] = total[g] * keep + add
+                peak[g][0] = top
+                mixed[g][0] = mixed[g][0] * keep + o_got[d, g].astype(jnp.float32) * add
+                total[g][0] = total[g][0] * keep + add
 
     for g in range(GROUP):
-        done[g] = (mixed[g] / total[g]).astype(jnp.bfloat16)
+        done[g] = (mixed[g][0] / total[g][0]).astype(jnp.bfloat16)
     for head in range(HEADS):
         out_all[:, head * HEAD : (head + 1) * HEAD] = done[place[head]]
     store = pltpu.make_async_copy(out_all, out, load_sem.at[5])
@@ -358,9 +414,9 @@
             pltpu.VMEM((2, 8, rows), f32),
             pltpu.VMEM((2, *heads), bf16),
             pltpu.VMEM((2, 8, rows), f32),
-            pltpu.VMEM((HEADS + 2 * GROUP, rows, LANES), f32),
-            pltpu.VMEM((HEADS + 2 * GROUP, rows, LANES), f32),
-            pltpu.VMEM((HEADS + 2 * GROUP, rows, HEAD), f32),
+            [pltpu.VMEM((5, rows, LANES), f32)] * GROUP,
+            [pltpu.VMEM((5, rows, LANES), f32)] * GROUP,
+            [pltpu.VMEM((5, rows, HEAD), f32)] * GROUP,
             pltpu.VMEM((HEADS, rows, HEAD), bf16),
             pltpu.SMEM((HEADS,), jnp.int32),
             pltpu.SMEM((HEADS,), jnp.int32),
@@ -371,7 +427,7 @@
             pltpu.SemaphoreType.DMA((5,)),
         ],
         compiler_params=pltpu.CompilerParams(
-            collective_id=0, has_side_effects=True, vmem_limit_bytes=50 << 20
+            collective_id=0, has_side_effects=True, vmem_limit_bytes=60 << 20
         ),
     )(
         query[0, 0], fresh_key[0, 0], fresh_value[0, 0], stale_kv[:, 0, 0], text_kv,

time: 88.4 us -> 79.2 us (0.90); the launches traced: 87.2 us -> 79 us
  Pallas kernels: 81.3 us -> 74.6 us
  local copies, waits for them, and re-layouts: 5.22 us -> 3.72 us
    pallas_call x1, Pallas kernels: 81.3 us -> 74.6 us  [on_device(): pl.pallas_call(kernel, out_shape=jax.ShapeDtypeStruct((rows, width), bf16...]
    unnamed x8 -> x2, local copies, waits for them, and re-layouts: 5.22 us -> 3.72 us
where the time goes in v2:
time: 79.2 us; the launch traced here: 79 us
  Pallas kernels  74.6 us (94%)
  local copies, waits for them, and re-layouts  3.72 us (5%)
    pallas_call x1, Pallas kernels, on_device(): pl.pallas_call(kernel, out_shape=jax.ShapeDtypeStruct((rows, width), bf16...  74.6 us
    unnamed x2, local copies, waits for them, and re-layouts  3.72 us

profile of v2, /device:TPU:1, one launch (start us, length us, event | category | flops | bytes accessed | tf_op | source)
XLA Modules:
  0.0 79.0 jit_solution(991822531533600607)
XLA Ops:
  0.7 1.4 %copy.8.window = s32[12,2]{1,0:T(8,128)} copy(s32[12,2]{0,1:T(2,128)} %param.12) | data formatting | bytes 192 | tf_op args[5]
  2.0 74.6 %shard_map.73 = bf16[384,1536]{1,0:T(8,128)(2,1)} custom-call(bf16[384,1536]{1,0:T(8,128)(2,1)} %bitcast.7, bf16[384,1536]{1,0:T(8,128)(2,1)} %bitcast.8, bf16[384,1536]{1,0:T(8,128)(2,1)} %bitcast.9, bf16[2,384,1536]{2,1,0:T(8,128)(2,1)} %bitcast.6, bf16[2,16,1536]{2,1,0:T(8,128)(2,1)} %text.1, s32[12,2]{1,0:T(8,128)} %copy.8.window, s32[1]{0:T(128)S(6)} %copy.10.text_len), custom_call_target="tpu_custom_call" | custom-call | tf_op jit(solution)/shard_map/pallas_call | solution.py:393
  76.6 2.4 %copy.11 = bf16[1,1,384,1536]{3,2,1,0:T(8,128)(2,1)} copy(bf16[1,1,384,1536]{3,2,1,0:T(8,128)(2,1)} %bitcast.5) | data formatting | bytes 2359296

commit v3 on v2

--- a/solution.py
+++ b/solution.py
@@ -23,7 +23,7 @@
     got11, got10, got01, gotq,
     o_send, o_stat, o_got, o_got_stat,
     peak, total, mixed, done, order, place,
-    load_sem, send_sem, recv_sem, text_send, text_recv,
+    relay, load_sem, send_sem, recv_sem, text_send, text_recv, relay_send, relay_recv,
 ):
     rows = q_all.shape[1]
     times = lax.axis_size("tm")
@@ -37,6 +37,15 @@
     has_space = (space > 0, space < spaces - 1)
     next_time = (time - 1, time + 1)
     next_space = (space - 1, space + 1)
+    middle = times // 2
+    first, last = time == 0, time == times - 1
+    outer = jnp.logical_or(first, last)
+    inner = jnp.logical_or(time == middle - 1, time == middle)
+    straight = (
+        jnp.logical_and(has_time[0], time != middle),
+        jnp.logical_and(has_time[1], time != middle - 1),
+    )
+    bent = (time == middle, time == middle - 1)
     scale = math.log2(math.e) / math.sqrt(HEAD)
 
     mine = words.at[core, column, low]
@@ -59,15 +68,27 @@
     partner_low = column * 4 + (1 - low) * 2 + core
     sibling = space + 1 - 2 * core
     barrier = pltpu.get_barrier_semaphore()
-    partners = [
-        {"tm": lax.rem(time + 1, times)},
-        {"tm": lax.rem(time + times - 1, times)},
-        {"space": lax.rem(space + 1, spaces)},
-        {"space": lax.rem(space + spaces - 1, spaces)},
-        {"space": partner_low},
-    ] + [{"space": lax.rem(space + 4 * d, spaces)} for d in (1, 2, 3)]
+    for d in (0, 1):
+        @pl.when(has_time[d])
+        def _():
+            pl.semaphore_signal(barrier, inc=1, device_id={"tm": time - 1 + 2 * d}, device_id_type=MESH)
+
+        @pl.when(has_space[d])
+        def _():
+            pl.semaphore_signal(barrier, inc=1, device_id={"space": space - 1 + 2 * d}, device_id_type=MESH)
+
+    partners = [partner_low] + [lax.rem(space + 4 * d, spaces) for d in (1, 2, 3)]
     for partner in partners:
-        pl.semaphore_signal(barrier, inc=1, device_id=partner, device_id_type=MESH)
+        pl.semaphore_signal(barrier, inc=1, device_id={"space": partner}, device_id_type=MESH)
+
+    @pl.when(jnp.logical_or(outer, inner))
+    def _():
+        for place_at in (0, 1):
+            partner = jnp.where(outer, middle - 1 + place_at, place_at * (times - 1))
+            pl.semaphore_signal(barrier, inc=1, device_id={"tm": partner}, device_id_type=MESH)
+
+    greeted = len(partners) + sum(has.astype(jnp.int32) for has in has_time + has_space)
+    greeted = greeted + 2 * jnp.logical_or(outer, inner).astype(jnp.int32)
 
     counts = [jnp.int32(0)] * 4
     slots = []
@@ -126,34 +147,54 @@
 
     loads[0].wait()
     pack(pack11, 0)
-    pl.semaphore_wait(barrier, len(partners))
+    pl.semaphore_wait(barrier, greeted)
     send_both(has_time, along_time, 0, pack11, got11)
-    loads[1].wait()
-    for g in range(GROUP):
-        packq[g] = q_all[order[g]]
-    send_both(has_space, along_space, 3, packq, gotq)
     loads[2].wait()
     swap = pltpu.make_async_remote_copy(
         src_ref=mine, dst_ref=mine, send_sem=text_send.at[0], recv_sem=text_recv.at[0],
         device_id={"space": partner_low}, device_id_type=MESH,
     )
     swap.start()
+    loads[1].wait()
+    for g in range(GROUP):
+        packq[g] = q_all[order[g]]
+    send_both(has_space, along_space, 3, packq, gotq)
     pack(pack01, 2 * GROUP)
     send_both(has_space, along_space, 2, pack01, got01)
     pack(pack10, GROUP)
-    send_both(has_time, along_time, 1, pack10, got10)
-
-    swap.wait_recv()
-    pair = words.at[core, column]
+
+    pieces = [(kv, g) for g in range(GROUP) for kv in range(2)]
+
+    def detour(d, i):
+        kv, g = pieces[i]
+        return pltpu.make_async_remote_copy(
+            src_ref=pack10.at[kv, g], dst_ref=relay.at[kv, g],
+            send_sem=send_sem.at[1, d], recv_sem=relay_recv.at[i],
+            device_id={"tm": (times - 1) * (1 - d)}, device_id_type=MESH,
+        )
+
+    def onward(d, i):
+        kv, g = pieces[i]
+        return pltpu.make_async_remote_copy(
+            src_ref=relay.at[kv, g], dst_ref=got10.at[1 - d, kv, g],
+            send_sem=relay_send, recv_sem=recv_sem.at[1, 1 - d],
+            device_id={"tm": middle - 1 + d}, device_id_type=MESH,
+        )
+
+    for d in (0, 1):
+        @pl.when(bent[d])
+        def _():
+            for i in range(len(pieces)):
+                detour(d, i).start()
+
     spread = [
         pltpu.make_async_remote_copy(
-            src_ref=pair, dst_ref=pair, send_sem=text_send.at[d], recv_sem=text_recv.at[d],
+            src_ref=words.at[core, column], dst_ref=words.at[core, column],
+            send_sem=text_send.at[d], recv_sem=text_recv.at[d],
             device_id={"space": lax.rem(space + 4 * d, spaces)}, device_id_type=MESH,
         )
         for d in (1, 2, 3)
     ]
-    for copy in spread:
-        copy.start()
 
     def rows_at(block):
         return pl.ds(block * ROW_BLOCK, ROW_BLOCK)
@@ -273,6 +314,10 @@
             for g in range(GROUP)
         ])
 
+    swap.wait_recv()
+    for copy in spread:
+        copy.start()
+
     arrived(has_space, along_space, 3, packq, gotq)
 
     def visitor(d, g):
@@ -286,6 +331,46 @@
                 job(visitor(d, g), [(pack11[0, g], pack11[1, g], None, None)], save(g, 3 + d))
                 for g in range(GROUP)
             ])
+
+    for d in (0, 1):
+        @pl.when(straight[d])
+        def _():
+            along_time(0, d, pack11, got11).wait_send()
+            along_time(1, d, pack10, got10).start()
+
+    for d, relaying in ((1, first), (0, last)):
+        @pl.when(relaying)
+        def _():
+            for i in range(len(pieces)):
+                detour(d, i).wait_recv()
+                onward(d, i).start()
+
+    arrived(has_time, along_time, 0, pack11, got11)
+    lane = lax.broadcasted_iota(jnp.int32, (rows, LANES), 1)
+
+    @pl.loop(0, 2)
+    def _(i):
+        d = lax.rem(i + core, 2)
+
+        @pl.when(side_ok(d, space, spaces))
+        def _():
+            def give(g):
+                def after(here, top, weight, value):
+                    o_send[d, g, here] = (value / weight).astype(jnp.bfloat16)
+                    peak[g][3 + d, here] = top + jnp.log2(weight)
+
+                return after
+
+            attend([
+                job(visitor(d, g), near(got11, g, has_time), give(g), saved(g, 3 + d))
+                for g in range(GROUP)
+            ])
+            stats = jnp.zeros((rows, LANES), jnp.float32)
+            for g in range(GROUP):
+                stats = jnp.where(lane == g, peak[g][3 + d], stats)
+            o_stat[d] = stats.T[:8]
+            along_space(4, d, o_send.at[d], o_got).start()
+            along_space(5, d, o_stat.at[d], o_got_stat).start()
 
     for copy in spread:
         copy.wait_recv()
@@ -300,33 +385,6 @@
         job(own(3 * GROUP + g), [fresh(3 * GROUP + g), spoken(3 * GROUP + g)], finish(done, (3 * GROUP + g,)))
         for g in range(GROUP)
     ])
-
-    arrived(has_time, along_time, 0, pack11, got11)
-    lane = lax.broadcasted_iota(jnp.int32, (rows, LANES), 1)
-
-    @pl.loop(0, 2)
-    def _(i):
-        d = lax.rem(i + core, 2)
-
-        @pl.when(side_ok(d, space, spaces))
-        def _():
-            def give(g):
-                def after(here, top, weight, value):
-                    o_send[d, g, here] = (value / weight).astype(jnp.bfloat16)
-                    peak[g][3 + d, here] = top + jnp.log2(weight)
-
-                return after
-
-            attend([
-                job(visitor(d, g), near(got11, g, has_time), give(g), saved(g, 3 + d))
-                for g in range(GROUP)
-            ])
-            stats = jnp.zeros((rows, LANES), jnp.float32)
-            for g in range(GROUP):
-                stats = jnp.where(lane == g, peak[g][3 + d], stats)
-            o_stat[d] = stats.T[:8]
-            along_space(4, d, o_send.at[d], o_got).start()
-            along_space(5, d, o_stat.at[d], o_got_stat).start()
 
     attend([
         job(own(g), [spoken(g), *near(got11, g, has_time)], save(g, 0), saved(g, 0))
@@ -367,8 +425,17 @@
     store = pltpu.make_async_copy(out_all, out, load_sem.at[5])
     store.start()
 
-    sent(has_time, along_time, 0, pack11, got11)
+    for d in (0, 1):
+        @pl.when(bent[d])
+        def _():
+            along_time(0, d, pack11, got11).wait_send()
+
     sent(has_time, along_time, 1, pack10, got10)
+
+    @pl.when(outer)
+    def _():
+        pltpu.make_async_copy(relay, relay, relay_send).wait()
+
     sent(has_space, along_space, 2, pack01, got01)
     sent(has_space, along_space, 3, packq, gotq)
     for d in (0, 1):
@@ -420,11 +487,14 @@
             pltpu.VMEM((HEADS, rows, HEAD), bf16),
             pltpu.SMEM((HEADS,), jnp.int32),
             pltpu.SMEM((HEADS,), jnp.int32),
+            pltpu.VMEM((2, *heads), bf16),
             pltpu.SemaphoreType.DMA((6,)),
             pltpu.SemaphoreType.DMA((6, 2)),
             pltpu.SemaphoreType.DMA((6, 2)),
             pltpu.SemaphoreType.DMA((5,)),
             pltpu.SemaphoreType.DMA((5,)),
+            pltpu.SemaphoreType.DMA(()),
+            pltpu.SemaphoreType.DMA((2 * GROUP,)),
         ],
         compiler_params=pltpu.CompilerParams(
             collective_id=0, has_side_effects=True, vmem_limit_bytes=60 << 20

time: 79.2 us -> 68.4 us (0.86)
  the two profiles are of different devices: /device:TPU:1 before, /device:TPU:3 now
where the time goes in v3:
time: 68.4 us; the launch traced here: 68.2 us
  Pallas kernels  63.8 us (93%)
  local copies, waits for them, and re-layouts  3.72 us (5%)
    pallas_call x1, Pallas kernels, on_device(): pl.pallas_call(kernel, out_shape=jax.ShapeDtypeStruct((rows, width), bf16...  63.8 us
    unnamed x2, local copies, waits for them, and re-layouts  3.72 us

profile of v3, /device:TPU:3, one launch (start us, length us, event | category | flops | bytes accessed | tf_op | source)
XLA Modules:
  0.0 68.2 jit_solution(14479954980550596897)
XLA Ops:
  0.7 1.4 %copy.8.window = s32[12,2]{1,0:T(8,128)} copy(s32[12,2]{0,1:T(2,128)} %param.12) | data formatting | bytes 192 | tf_op args[5]
  2.0 63.8 %shard_map.73 = bf16[384,1536]{1,0:T(8,128)(2,1)} custom-call(bf16[384,1536]{1,0:T(8,128)(2,1)} %bitcast.7, bf16[384,1536]{1,0:T(8,128)(2,1)} %bitcast.8, bf16[384,1536]{1,0:T(8,128)(2,1)} %bitcast.9, bf16[2,384,1536]{2,1,0:T(8,128)(2,1)} %bitcast.6, bf16[2,16,1536]{2,1,0:T(8,128)(2,1)} %text.1, s32[12,2]{1,0:T(8,128)} %copy.8.window, s32[1]{0:T(128)S(6)} %copy.10.text_len), custom_call_target="tpu_custom_call" | custom-call | tf_op jit(solution)/shard_map/pallas_call | solution.py:460
  65.9 2.4 %copy.11 = bf16[1,1,384,1536]{3,2,1,0:T(8,128)(2,1)} copy(bf16[1,1,384,1536]{3,2,1,0:T(8,128)(2,1)} %bitcast.5) | data formatting | bytes 2359296

commit v4 on v3

--- a/solution.py
+++ b/solution.py
@@ -16,14 +16,42 @@
 ROW_BLOCK = 384
 
 
+def slots_of(window):
+    counts = [jnp.int32(0)] * 4
+    slots = []
+    for head in range(HEADS):
+        reach_time, reach_space = window[0, head], window[1, head]
+        both = reach_time * reach_space
+        hits = [both, reach_time - both, reach_space - both, 1 - reach_time - reach_space + both]
+        slot = jnp.int32(0)
+        for k in range(4):
+            slot = slot + hits[k] * (GROUP * k + counts[k])
+            counts[k] = counts[k] + hits[k]
+        slots.append(slot)
+    return slots
+
+
+def arrange(by_slot, window, out, sems):
+    copies = [
+        pltpu.make_async_copy(
+            by_slot.at[jnp.minimum(slot, HEADS - 1)], out.at[:, pl.ds(head * HEAD, HEAD)], sems.at[head]
+        )
+        for head, slot in enumerate(slots_of(window))
+    ]
+    for copy in copies:
+        copy.start()
+    for copy in copies:
+        copy.wait()
+
+
 def kernel(
     query, fresh_key, fresh_value, stale, text, window, text_len, out,
-    q_all, k_all, v_all, stale_all, words, out_all,
+    q_all, k_all, v_all, stale_all, words,
     pack11, pack10, pack01, packq,
     got11, got10, got01, gotq,
     o_send, o_stat, o_got, o_got_stat,
-    peak, total, mixed, done, order, place,
-    relay, load_sem, send_sem, recv_sem, text_send, text_recv, relay_send, relay_recv,
+    peak, total, mixed, done, order,
+    relay, load_sem, send_sem, recv_sem, text_send, text_recv, relay_send, relay_recv, store_sem,
 ):
     rows = q_all.shape[1]
     times = lax.axis_size("tm")
@@ -90,18 +118,7 @@
     greeted = len(partners) + sum(has.astype(jnp.int32) for has in has_time + has_space)
     greeted = greeted + 2 * jnp.logical_or(outer, inner).astype(jnp.int32)
 
-    counts = [jnp.int32(0)] * 4
-    slots = []
-    for head in range(HEADS):
-        reach_time, reach_space = window[head, 0], window[head, 1]
-        both = reach_time * reach_space
-        hits = [both, reach_time - both, reach_space - both, 1 - reach_time - reach_space + both]
-        slot = jnp.int32(0)
-        for k in range(4):
-            slot = slot + hits[k] * (GROUP * k + counts[k])
-            counts[k] = counts[k] + hits[k]
-        slots.append(slot)
-        place[head] = jnp.minimum(slot, HEADS - 1)
+    slots = slots_of(window)
     for s in range(HEADS):
         chosen = jnp.int32(0)
         for head in range(HEADS):
@@ -160,7 +177,6 @@
         packq[g] = q_all[order[g]]
     send_both(has_space, along_space, 3, packq, gotq)
     pack(pack01, 2 * GROUP)
-    send_both(has_space, along_space, 2, pack01, got01)
     pack(pack10, GROUP)
 
     pieces = [(kv, g) for g in range(GROUP) for kv in range(2)]
@@ -195,6 +211,13 @@
         )
         for d in (1, 2, 3)
     ]
+
+    def stored(kind):
+        here = pl.ds(kind * GROUP, GROUP)
+        return pltpu.make_async_copy(done.at[here], out.at[here], store_sem.at[kind])
+
+    def store_kind(kind):
+        stored(kind).start()
 
     def rows_at(block):
         return pl.ds(block * ROW_BLOCK, ROW_BLOCK)
@@ -332,6 +355,11 @@
                 for g in range(GROUP)
             ])
 
+    def send_sides():
+        send_both(has_space, along_space, 2, pack01, got01)
+
+    pl.when(jnp.logical_not(outer))(send_sides)
+
     for d in (0, 1):
         @pl.when(straight[d])
         def _():
@@ -371,6 +399,8 @@
             o_stat[d] = stats.T[:8]
             along_space(4, d, o_send.at[d], o_got).start()
             along_space(5, d, o_stat.at[d], o_got_stat).start()
+
+    pl.when(outer)(send_sides)
 
     for copy in spread:
         copy.wait_recv()
@@ -385,6 +415,7 @@
         job(own(3 * GROUP + g), [fresh(3 * GROUP + g), spoken(3 * GROUP + g)], finish(done, (3 * GROUP + g,)))
         for g in range(GROUP)
     ])
+    store_kind(3)
 
     attend([
         job(own(g), [spoken(g), *near(got11, g, has_time)], save(g, 0), saved(g, 0))
@@ -395,11 +426,13 @@
         job(own(2 * GROUP + g), [spoken(2 * GROUP + g), *near(got01, g, has_space)], finish(done, (2 * GROUP + g,)), saved(g, 2))
         for g in range(GROUP)
     ])
+    store_kind(2)
     arrived(has_time, along_time, 1, pack10, got10)
     attend([
         job(own(GROUP + g), [spoken(GROUP + g), *near(got10, g, has_time)], finish(done, (GROUP + g,)), saved(g, 1))
         for g in range(GROUP)
     ])
+    store_kind(1)
 
     for d in (0, 1):
         @pl.when(has_space[d])
@@ -420,10 +453,7 @@
 
     for g in range(GROUP):
         done[g] = (mixed[g][0] / total[g][0]).astype(jnp.bfloat16)
-    for head in range(HEADS):
-        out_all[:, head * HEAD : (head + 1) * HEAD] = done[place[head]]
-    store = pltpu.make_async_copy(out_all, out, load_sem.at[5])
-    store.start()
+    store_kind(0)
 
     for d in (0, 1):
         @pl.when(bent[d])
@@ -447,7 +477,8 @@
     for copy in spread:
         copy.wait_send()
     across.wait_send()
-    store.wait()
+    for kind in range(4):
+        stored(kind).wait()
 
 
 def on_device(query, fresh_key, fresh_value, stale_kv, text_kv, window, text_len):
@@ -457,9 +488,9 @@
     heads = (GROUP, rows, HEAD)
     anywhere = pl.BlockSpec(memory_space=pl.ANY)
     scalars = pl.BlockSpec(memory_space=pltpu.SMEM)
-    result = pl.pallas_call(
+    by_slot = pl.pallas_call(
         kernel,
-        out_shape=jax.ShapeDtypeStruct((rows, width), bf16),
+        out_shape=jax.ShapeDtypeStruct((HEADS, rows, HEAD), bf16),
         in_specs=[anywhere] * 5 + [scalars] * 2,
         out_specs=anywhere,
         scratch_shapes=[
@@ -468,7 +499,6 @@
             pltpu.VMEM((HEADS, rows, HEAD), bf16),
             pltpu.VMEM((HEADS, 2, rows, HEAD), bf16),
             pltpu.VMEM((2, 4, 2, HEADS, 2, words, HEAD), bf16),
-            pltpu.VMEM((rows, width), bf16),
             pltpu.VMEM((2, *heads), bf16),
             pltpu.VMEM((2, *heads), bf16),
             pltpu.VMEM((2, *heads), bf16),
@@ -486,23 +516,31 @@
             [pltpu.VMEM((5, rows, HEAD), f32)] * GROUP,
             pltpu.VMEM((HEADS, rows, HEAD), bf16),
             pltpu.SMEM((HEADS,), jnp.int32),
-            pltpu.SMEM((HEADS,), jnp.int32),
-            pltpu.VMEM((2, *heads), bf16),
-            pltpu.SemaphoreType.DMA((6,)),
+            pltpu.VMEM((2, *heads), bf16),
+            pltpu.SemaphoreType.DMA((5,)),
             pltpu.SemaphoreType.DMA((6, 2)),
             pltpu.SemaphoreType.DMA((6, 2)),
             pltpu.SemaphoreType.DMA((5,)),
             pltpu.SemaphoreType.DMA((5,)),
             pltpu.SemaphoreType.DMA(()),
             pltpu.SemaphoreType.DMA((2 * GROUP,)),
+            pltpu.SemaphoreType.DMA((4,)),
         ],
         compiler_params=pltpu.CompilerParams(
             collective_id=0, has_side_effects=True, vmem_limit_bytes=60 << 20
         ),
     )(
         query[0, 0], fresh_key[0, 0], fresh_value[0, 0], stale_kv[:, 0, 0], text_kv,
-        window, text_len,
+        window.T, text_len,
     )
+    result = pl.pallas_call(
+        arrange,
+        out_shape=jax.ShapeDtypeStruct((rows, width), bf16),
+        in_specs=[anywhere, scalars],
+        out_specs=anywhere,
+        scratch_shapes=[pltpu.SemaphoreType.DMA((HEADS,))],
+        compiler_params=pltpu.CompilerParams(vmem_limit_bytes=60 << 20),
+    )(by_slot, window.T)
     return result[None, None]
 
 

time: 68.4 us -> 109 us (1.59)
  the two profiles are of different devices: /device:TPU:3 before, /device:TPU:10 now
where the time goes in v4:
time: 109 us
  Pallas kernels  108 us (99%)
    pallas_call x1, Pallas kernels, on_device(): pl.pallas_call(kernel, out_shape=jax.ShapeDtypeStruct((HEADS, rows, HEAD)...  70.5 us
    pallas_call x1, Pallas kernels, on_device(): pl.pallas_call(arrange, out_shape=jax.ShapeDtypeStruct((rows, width), bf1...  37.6 us

profile of v4, /device:TPU:10, one launch (start us, length us, event | category | flops | bytes accessed | tf_op | source)
XLA Modules:
  0.0 108.8 jit_solution(2254076177764524837)
XLA Ops:
  0.7 70.5 %shard_map.73.by_slot = bf16[12,384,128]{2,1,0:T(8,128)(2,1)} custom-call(bf16[384,1536]{1,0:T(8,128)(2,1)} %bitcast.7, bf16[384,1536]{1,0:T(8,128)(2,1)} %bitcast.8, bf16[384,1536]{1,0:T(8,128)(2,1)} %bitcast.9, bf16[2,384,1536]{2,1,0:T(8,128)(2,1)} %bitcast.6, bf16[2,16,1536]{2,1,0:T(8,128)(2,1)} %text.1, s32[2,12]{1,0:T(2,128)} %bitcast.10, ...), custom_call_target="tpu_custom_call" | custom-call | tf_op jit(solution)/shard_map/pallas_call | solution.py:491
  71.2 37.6 %shard_map.74 = bf16[384,1536]{1,0:T(8,128)(2,1)} custom-call(bf16[12,384,128]{2,1,0:T(8,128)(2,1)} %shard_map.73.by_slot, s32[2,12]{1,0:T(2,128)} %bitcast.11), custom_call_target="tpu_custom_call" | custom-call | tf_op jit(solution)/shard_map/pallas_call | solution.py:536

commit v5 on v4

--- a/solution.py
+++ b/solution.py
@@ -31,17 +31,20 @@
     return slots
 
 
-def arrange(by_slot, window, out, sems):
-    copies = [
-        pltpu.make_async_copy(
-            by_slot.at[jnp.minimum(slot, HEADS - 1)], out.at[:, pl.ds(head * HEAD, HEAD)], sems.at[head]
-        )
-        for head, slot in enumerate(slots_of(window))
-    ]
-    for copy in copies:
-        copy.start()
-    for copy in copies:
-        copy.wait()
+def arrange(by_slot, window, out, staged, load_sem, store_sem):
+    loads, stores = [], []
+    for head, slot in enumerate(slots_of(window)):
+        source = by_slot.at[jnp.minimum(slot, HEADS - 1)]
+        target = out.at[:, pl.ds(head * HEAD, HEAD)]
+        loads.append(pltpu.make_async_copy(source, staged.at[head], load_sem.at[head]))
+        stores.append(pltpu.make_async_copy(staged.at[head], target, store_sem.at[head]))
+    for load in loads:
+        load.start()
+    for load, store in zip(loads, stores):
+        load.wait()
+        store.start()
+    for store in stores:
+        store.wait()
 
 
 def kernel(
@@ -66,8 +69,6 @@
     next_time = (time - 1, time + 1)
     next_space = (space - 1, space + 1)
     middle = times // 2
-    first, last = time == 0, time == times - 1
-    outer = jnp.logical_or(first, last)
     inner = jnp.logical_or(time == middle - 1, time == middle)
     straight = (
         jnp.logical_and(has_time[0], time != middle),
@@ -109,14 +110,13 @@
     for partner in partners:
         pl.semaphore_signal(barrier, inc=1, device_id={"space": partner}, device_id_type=MESH)
 
-    @pl.when(jnp.logical_or(outer, inner))
+    @pl.when(inner)
     def _():
-        for place_at in (0, 1):
-            partner = jnp.where(outer, middle - 1 + place_at, place_at * (times - 1))
-            pl.semaphore_signal(barrier, inc=1, device_id={"tm": partner}, device_id_type=MESH)
+        opposite = {"tm": 2 * middle - 1 - time, "space": partner_low}
+        pl.semaphore_signal(barrier, inc=1, device_id=opposite, device_id_type=MESH)
 
     greeted = len(partners) + sum(has.astype(jnp.int32) for has in has_time + has_space)
-    greeted = greeted + 2 * jnp.logical_or(outer, inner).astype(jnp.int32)
+    greeted = greeted + inner.astype(jnp.int32)
 
     slots = slots_of(window)
     for s in range(HEADS):
@@ -176,7 +176,6 @@
     for g in range(GROUP):
         packq[g] = q_all[order[g]]
     send_both(has_space, along_space, 3, packq, gotq)
-    pack(pack01, 2 * GROUP)
     pack(pack10, GROUP)
 
     pieces = [(kv, g) for g in range(GROUP) for kv in range(2)]
@@ -186,7 +185,7 @@
         return pltpu.make_async_remote_copy(
             src_ref=pack10.at[kv, g], dst_ref=relay.at[kv, g],
             send_sem=send_sem.at[1, d], recv_sem=relay_recv.at[i],
-            device_id={"tm": (times - 1) * (1 - d)}, device_id_type=MESH,
+            device_id={"space": partner_low}, device_id_type=MESH,
         )
 
     def onward(d, i):
@@ -194,7 +193,7 @@
         return pltpu.make_async_remote_copy(
             src_ref=relay.at[kv, g], dst_ref=got10.at[1 - d, kv, g],
             send_sem=relay_send, recv_sem=recv_sem.at[1, 1 - d],
-            device_id={"tm": middle - 1 + d}, device_id_type=MESH,
+            device_id={"tm": time - 1 + 2 * d, "space": partner_low}, device_id_type=MESH,
         )
 
     for d in (0, 1):
@@ -202,6 +201,9 @@
         def _():
             for i in range(len(pieces)):
                 detour(d, i).start()
+
+    pack(pack01, 2 * GROUP)
+    send_both(has_space, along_space, 2, pack01, got01)
 
     spread = [
         pltpu.make_async_remote_copy(
@@ -355,19 +357,14 @@
                 for g in range(GROUP)
             ])
 
-    def send_sides():
-        send_both(has_space, along_space, 2, pack01, got01)
-
-    pl.when(jnp.logical_not(outer))(send_sides)
-
     for d in (0, 1):
         @pl.when(straight[d])
         def _():
             along_time(0, d, pack11, got11).wait_send()
             along_time(1, d, pack10, got10).start()
 
-    for d, relaying in ((1, first), (0, last)):
-        @pl.when(relaying)
+    for d in (0, 1):
+        @pl.when(bent[d])
         def _():
             for i in range(len(pieces)):
                 detour(d, i).wait_recv()
@@ -399,8 +396,6 @@
             o_stat[d] = stats.T[:8]
             along_space(4, d, o_send.at[d], o_got).start()
             along_space(5, d, o_stat.at[d], o_got_stat).start()
-
-    pl.when(outer)(send_sides)
 
     for copy in spread:
         copy.wait_recv()
@@ -462,7 +457,7 @@
 
     sent(has_time, along_time, 1, pack10, got10)
 
-    @pl.when(outer)
+    @pl.when(inner)
     def _():
         pltpu.make_async_copy(relay, relay, relay_send).wait()
 
@@ -538,7 +533,11 @@
         out_shape=jax.ShapeDtypeStruct((rows, width), bf16),
         in_specs=[anywhere, scalars],
         out_specs=anywhere,
-        scratch_shapes=[pltpu.SemaphoreType.DMA((HEADS,))],
+        scratch_shapes=[
+            pltpu.VMEM((HEADS, rows, HEAD), bf16),
+            pltpu.SemaphoreType.DMA((HEADS,)),
+            pltpu.SemaphoreType.DMA((HEADS,)),
+        ],
         compiler_params=pltpu.CompilerParams(vmem_limit_bytes=60 << 20),
     )(by_slot, window.T)
     return result[None, None]

time: 109 us -> 60.1 us (0.55)
  the two profiles are of different devices: /device:TPU:10 before, /device:TPU:1 now
where the time goes in v5:
time: 60.1 us; the launch traced here: 60 us
  Pallas kernels  59.3 us (99%)
  between operations  0.66 us (1%)
    pallas_call x1, Pallas kernels, on_device(): pl.pallas_call(kernel, out_shape=jax.ShapeDtypeStruct((HEADS, rows, HEAD)...  56.4 us
    pallas_call x1, Pallas kernels, on_device(): pl.pallas_call(arrange, out_shape=jax.ShapeDtypeStruct((rows, width), bf1...  2.9 us

profile of v5, /device:TPU:1, one launch (start us, length us, event | category | flops | bytes accessed | tf_op | source)
XLA Modules:
  0.0 60.0 jit_solution(17189045523035001080)
XLA Ops:
  0.7 56.4 %shard_map.73.by_slot = bf16[12,384,128]{2,1,0:T(8,128)(2,1)} custom-call(bf16[384,1536]{1,0:T(8,128)(2,1)} %bitcast.7, bf16[384,1536]{1,0:T(8,128)(2,1)} %bitcast.8, bf16[384,1536]{1,0:T(8,128)(2,1)} %bitcast.9, bf16[2,384,1536]{2,1,0:T(8,128)(2,1)} %bitcast.6, bf16[2,16,1536]{2,1,0:T(8,128)(2,1)} %text.1, s32[2,12]{1,0:T(2,128)} %bitcast.10, ...), custom_call_target="tpu_custom_call" | custom-call | tf_op jit(solution)/shard_map/pallas_call | solution.py:486
  57.1 2.9 %shard_map.74 = bf16[384,1536]{1,0:T(8,128)(2,1)} custom-call(bf16[12,384,128]{2,1,0:T(8,128)(2,1)} %shard_map.73.by_slot, s32[2,12]{1,0:T(2,128)} %bitcast.11), custom_call_target="tpu_custom_call" | custom-call | tf_op jit(solution)/shard_map/pallas_call | solution.py:531

commit v6 on v3

--- a/solution.py
+++ b/solution.py
@@ -16,16 +16,33 @@
 ROW_BLOCK = 384
 
 
+def slots_of(window):
+    counts = [jnp.int32(0)] * 4
+    slots = []
+    for head in range(HEADS):
+        reach_time, reach_space = window[0, head], window[1, head]
+        both = reach_time * reach_space
+        hits = [both, reach_time - both, reach_space - both, 1 - reach_time - reach_space + both]
+        slot = jnp.int32(0)
+        for k in range(4):
+            slot = slot + hits[k] * (GROUP * k + counts[k])
+            counts[k] = counts[k] + hits[k]
+        slots.append(slot)
+    return slots
+
+
 def kernel(
     query, fresh_key, fresh_value, stale, text, window, text_len, out,
     q_all, k_all, v_all, stale_all, words, out_all,
-    pack11, pack10, pack01, packq,
-    got11, got10, got01, gotq,
+    pack11, sides, packq,
+    got11, got_sides, gotq,
     o_send, o_stat, o_got, o_got_stat,
     peak, total, mixed, done, order, place,
     relay, load_sem, send_sem, recv_sem, text_send, text_recv, relay_send, relay_recv,
 ):
     rows = q_all.shape[1]
+    pack10, pack01 = sides.at[0], sides.at[1]
+    got10, got01 = got_sides.at[0], got_sides.at[1]
     times = lax.axis_size("tm")
     spaces = lax.axis_size("space")
     time = lax.axis_index("tm")
@@ -38,8 +55,6 @@
     next_time = (time - 1, time + 1)
     next_space = (space - 1, space + 1)
     middle = times // 2
-    first, last = time == 0, time == times - 1
-    outer = jnp.logical_or(first, last)
     inner = jnp.logical_or(time == middle - 1, time == middle)
     straight = (
         jnp.logical_and(has_time[0], time != middle),
@@ -49,17 +64,13 @@
     scale = math.log2(math.e) / math.sqrt(HEAD)
 
     mine = words.at[core, column, low]
-    for head in range(HEADS):
-        at = pl.ds(head * HEAD, HEAD)
+    lanes = [pl.ds(head * HEAD, HEAD) for head in range(HEADS)]
+    for head, at in enumerate(lanes):
+        pltpu.make_async_copy(text.at[:, :, at], mine.at[head], load_sem.at[2]).start()
+    for head, at in enumerate(lanes):
         pltpu.make_async_copy(stale.at[:, :, at], stale_all.at[head], load_sem.at[0]).start()
-    for head in range(HEADS):
-        at = pl.ds(head * HEAD, HEAD)
+    for head, at in enumerate(lanes):
         pltpu.make_async_copy(query.at[:, at], q_all.at[head], load_sem.at[1]).start()
-        pltpu.make_async_copy(text.at[:, :, at], mine.at[head], load_sem.at[2]).start()
-    for head in range(HEADS):
-        at = pl.ds(head * HEAD, HEAD)
-        pltpu.make_async_copy(fresh_key.at[:, at], k_all.at[head], load_sem.at[3]).start()
-        pltpu.make_async_copy(fresh_value.at[:, at], v_all.at[head], load_sem.at[4]).start()
     loads = [
         pltpu.make_async_copy(target, target, load_sem.at[i])
         for i, target in enumerate((stale_all, q_all, mine, k_all, v_all))
@@ -81,27 +92,17 @@
     for partner in partners:
         pl.semaphore_signal(barrier, inc=1, device_id={"space": partner}, device_id_type=MESH)
 
-    @pl.when(jnp.logical_or(outer, inner))
+    @pl.when(inner)
     def _():
-        for place_at in (0, 1):
-            partner = jnp.where(outer, middle - 1 + place_at, place_at * (times - 1))
-            pl.semaphore_signal(barrier, inc=1, device_id={"tm": partner}, device_id_type=MESH)
+        opposite = {"tm": 2 * middle - 1 - time, "space": partner_low}
+        pl.semaphore_signal(barrier, inc=1, device_id=opposite, device_id_type=MESH)
 
     greeted = len(partners) + sum(has.astype(jnp.int32) for has in has_time + has_space)
-    greeted = greeted + 2 * jnp.logical_or(outer, inner).astype(jnp.int32)
-
-    counts = [jnp.int32(0)] * 4
-    slots = []
+    greeted = greeted + inner.astype(jnp.int32)
+
+    slots = slots_of(window)
     for head in range(HEADS):
-        reach_time, reach_space = window[head, 0], window[head, 1]
-        both = reach_time * reach_space
-        hits = [both, reach_time - both, reach_space - both, 1 - reach_time - reach_space + both]
-        slot = jnp.int32(0)
-        for k in range(4):
-            slot = slot + hits[k] * (GROUP * k + counts[k])
-            counts[k] = counts[k] + hits[k]
-        slots.append(slot)
-        place[head] = jnp.minimum(slot, HEADS - 1)
+        place[head] = jnp.minimum(slots[head], HEADS - 1)
     for s in range(HEADS):
         chosen = jnp.int32(0)
         for head in range(HEADS):
@@ -144,48 +145,6 @@
             @pl.when(has[d])
             def _():
                 make(kind, d, source, target).wait_send()
-
-    loads[0].wait()
-    pack(pack11, 0)
-    pl.semaphore_wait(barrier, greeted)
-    send_both(has_time, along_time, 0, pack11, got11)
-    loads[2].wait()
-    swap = pltpu.make_async_remote_copy(
-        src_ref=mine, dst_ref=mine, send_sem=text_send.at[0], recv_sem=text_recv.at[0],
-        device_id={"space": partner_low}, device_id_type=MESH,
-    )
-    swap.start()
-    loads[1].wait()
-    for g in range(GROUP):
-        packq[g] = q_all[order[g]]
-    send_both(has_space, along_space, 3, packq, gotq)
-    pack(pack01, 2 * GROUP)
-    send_both(has_space, along_space, 2, pack01, got01)
-    pack(pack10, GROUP)
-
-    pieces = [(kv, g) for g in range(GROUP) for kv in range(2)]
-
-    def detour(d, i):
-        kv, g = pieces[i]
-        return pltpu.make_async_remote_copy(
-            src_ref=pack10.at[kv, g], dst_ref=relay.at[kv, g],
-            send_sem=send_sem.at[1, d], recv_sem=relay_recv.at[i],
-            device_id={"tm": (times - 1) * (1 - d)}, device_id_type=MESH,
-        )
-
-    def onward(d, i):
-        kv, g = pieces[i]
-        return pltpu.make_async_remote_copy(
-            src_ref=relay.at[kv, g], dst_ref=got10.at[1 - d, kv, g],
-            send_sem=relay_send, recv_sem=recv_sem.at[1, 1 - d],
-            device_id={"tm": middle - 1 + d}, device_id_type=MESH,
-        )
-
-    for d in (0, 1):
-        @pl.when(bent[d])
-        def _():
-            for i in range(len(pieces)):
-                detour(d, i).start()
 
     spread = [
         pltpu.make_async_remote_copy(
@@ -195,6 +154,54 @@
         )
         for d in (1, 2, 3)
     ]
+    swap = pltpu.make_async_remote_copy(
+        src_ref=mine, dst_ref=mine, send_sem=text_send.at[0], recv_sem=text_recv.at[0],
+        device_id={"space": partner_low}, device_id_type=MESH,
+    )
+    loads[2].wait()
+    pl.semaphore_wait(barrier, greeted)
+    swap.start()
+    loads[0].wait()
+    pack(pack11, 0)
+    send_both(has_time, along_time, 0, pack11, got11)
+    for head, at in enumerate(lanes):
+        pltpu.make_async_copy(fresh_key.at[:, at], k_all.at[head], load_sem.at[3]).start()
+        pltpu.make_async_copy(fresh_value.at[:, at], v_all.at[head], load_sem.at[4]).start()
+    swap.wait_recv()
+    for copy in spread:
+        copy.start()
+    loads[1].wait()
+    for g in range(GROUP):
+        packq[g] = q_all[order[g]]
+    send_both(has_space, along_space, 3, packq, gotq)
+    pack(pack10, GROUP)
+
+    pieces = [(kv, g) for g in range(GROUP) for kv in range(2)]
+
+    def detour(d, i):
+        kv, g = pieces[i]
+        return pltpu.make_async_remote_copy(
+            src_ref=pack10.at[kv, g], dst_ref=relay.at[kv, g],
+            send_sem=send_sem.at[1, d], recv_sem=relay_recv.at[i],
+            device_id={"space": partner_low}, device_id_type=MESH,
+        )
+
+    def onward(d, i):
+        kv, g = pieces[i]
+        return pltpu.make_async_remote_copy(
+            src_ref=relay.at[kv, g], dst_ref=got10.at[1 - d, kv, g],
+            send_sem=relay_send, recv_sem=recv_sem.at[1, 1 - d],
+            device_id={"tm": time - 1 + 2 * d, "space": partner_low}, device_id_type=MESH,
+        )
+
+    for d in (0, 1):
+        @pl.when(bent[d])
+        def _():
+            for i in range(len(pieces)):
+                detour(d, i).start()
+
+    pack(pack01, 2 * GROUP)
+    send_both(has_space, along_space, 2, pack01, got01)
 
     def rows_at(block):
         return pl.ds(block * ROW_BLOCK, ROW_BLOCK)
@@ -303,6 +310,8 @@
         @pl.when(jnp.logical_not(has_space[d]))
         def _():
             got01[d] = jnp.zeros_like(got01[d])
+            o_got[d] = jnp.zeros_like(o_got[d])
+            o_got_stat[d] = jnp.full_like(o_got_stat[d], -1e30)
 
     loads[3].wait()
     loads[4].wait()
@@ -314,10 +323,6 @@
             for g in range(GROUP)
         ])
 
-    swap.wait_recv()
-    for copy in spread:
-        copy.start()
-
     arrived(has_space, along_space, 3, packq, gotq)
 
     def visitor(d, g):
@@ -338,8 +343,17 @@
             along_time(0, d, pack11, got11).wait_send()
             along_time(1, d, pack10, got10).start()
 
-    for d, relaying in ((1, first), (0, last)):
-        @pl.when(relaying)
+    for copy in spread:
+        copy.wait_recv()
+    half = words.at[core]
+    across = pltpu.make_async_remote_copy(
+        src_ref=half, dst_ref=half, send_sem=text_send.at[4], recv_sem=text_recv.at[4],
+        device_id={"space": sibling}, device_id_type=MESH,
+    )
+    across.start()
+
+    for d in (0, 1):
+        @pl.when(bent[d])
         def _():
             for i in range(len(pieces)):
                 detour(d, i).wait_recv()
@@ -372,14 +386,6 @@
             along_space(4, d, o_send.at[d], o_got).start()
             along_space(5, d, o_stat.at[d], o_got_stat).start()
 
-    for copy in spread:
-        copy.wait_recv()
-    half = words.at[core]
-    across = pltpu.make_async_remote_copy(
-        src_ref=half, dst_ref=half, send_sem=text_send.at[4], recv_sem=text_recv.at[4],
-        device_id={"space": sibling}, device_id_type=MESH,
-    )
-    across.start()
     across.wait_recv()
     attend([
         job(own(3 * GROUP + g), [fresh(3 * GROUP + g), spoken(3 * GROUP + g)], finish(done, (3 * GROUP + g,)))
@@ -390,36 +396,51 @@
         job(own(g), [spoken(g), *near(got11, g, has_time)], save(g, 0), saved(g, 0))
         for g in range(GROUP)
     ])
-    arrived(has_space, along_space, 2, pack01, got01)
-    attend([
-        job(own(2 * GROUP + g), [spoken(2 * GROUP + g), *near(got01, g, has_space)], finish(done, (2 * GROUP + g,)), saved(g, 2))
-        for g in range(GROUP)
-    ])
-    arrived(has_time, along_time, 1, pack10, got10)
-    attend([
-        job(own(GROUP + g), [spoken(GROUP + g), *near(got10, g, has_time)], finish(done, (GROUP + g,)), saved(g, 1))
-        for g in range(GROUP)
-    ])
-
+    outer = jnp.logical_or(time == 0, time == times - 1)
+
+    @pl.loop(0, 2)
+    def _(i):
+        k = jnp.where(outer, i, 1 - i)
+
+        @pl.when(k == 0)
+        def _():
+            arrived(has_time, along_time, 1, pack10, got10)
+
+        @pl.when(k == 1)
+        def _():
+            arrived(has_space, along_space, 2, pack01, got01)
+
+        valid = [jnp.where(k == 0, has_time[e], has_space[e]) for e in (0, 1)]
+        attend([
+            job(
+                own((1 + k) * GROUP + g),
+                [spoken((1 + k) * GROUP + g)]
+                + [(got_sides[k, e, 0, g], got_sides[k, e, 1, g], None, valid[e]) for e in (0, 1)],
+                finish(done, ((1 + k) * GROUP + g,)),
+                saved(g, 1 + k),
+            )
+            for g in range(GROUP)
+        ])
+
+    logs = []
     for d in (0, 1):
         @pl.when(has_space[d])
         def _():
             along_space(4, 1 - d, o_send.at[1 - d], o_got).wait_recv()
             along_space(5, 1 - d, o_stat.at[1 - d], o_got_stat).wait_recv()
-            spare = jnp.zeros((LANES - 8, rows), jnp.float32)
-            stats = jnp.concatenate([o_got_stat[d], spare], axis=0).T
-            for g in range(GROUP):
-                other = jnp.broadcast_to(stats[:, g : g + 1], (rows, LANES))
-                before = peak[g][0]
-                top = jnp.maximum(before, other)
-                keep = jnp.exp2(before - top)
-                add = jnp.exp2(other - top)
-                peak[g][0] = top
-                mixed[g][0] = mixed[g][0] * keep + o_got[d, g].astype(jnp.float32) * add
-                total[g][0] = total[g][0] * keep + add
-
+
+        spare = jnp.zeros((LANES - 8, rows), jnp.float32)
+        logs.append(jnp.concatenate([o_got_stat[d], spare], axis=0).T)
     for g in range(GROUP):
-        done[g] = (mixed[g][0] / total[g][0]).astype(jnp.bfloat16)
+        others = [jnp.broadcast_to(log[:, g : g + 1], (rows, LANES)) for log in logs]
+        top = jnp.maximum(peak[g][0], jnp.maximum(*others))
+        keep = jnp.exp2(peak[g][0] - top)
+        add = [jnp.exp2(other - top) for other in others]
+        value = mixed[g][0] * keep
+        for d in (0, 1):
+            value = value + o_got[d, g].astype(jnp.float32) * add[d]
+        done[g] = (value / (total[g][0] * keep + add[0] + add[1])).astype(jnp.bfloat16)
+
     for head in range(HEADS):
         out_all[:, head * HEAD : (head + 1) * HEAD] = done[place[head]]
     store = pltpu.make_async_copy(out_all, out, load_sem.at[5])
@@ -432,7 +453,7 @@
 
     sent(has_time, along_time, 1, pack10, got10)
 
-    @pl.when(outer)
+    @pl.when(inner)
     def _():
         pltpu.make_async_copy(relay, relay, relay_send).wait()
 
@@ -455,13 +476,12 @@
     words = text_kv.shape[1]
     bf16, f32 = jnp.bfloat16, jnp.float32
     heads = (GROUP, rows, HEAD)
-    anywhere = pl.BlockSpec(memory_space=pl.ANY)
     scalars = pl.BlockSpec(memory_space=pltpu.SMEM)
     result = pl.pallas_call(
         kernel,
         out_shape=jax.ShapeDtypeStruct((rows, width), bf16),
-        in_specs=[anywhere] * 5 + [scalars] * 2,
-        out_specs=anywhere,
+        in_specs=[pl.BlockSpec(memory_space=pltpu.HBM)] * 5 + [scalars] * 2,
+        out_specs=pl.BlockSpec(memory_space=pl.ANY),
         scratch_shapes=[
             pltpu.VMEM((HEADS, rows, HEAD), bf16),
             pltpu.VMEM((HEADS, rows, HEAD), bf16),
@@ -470,12 +490,10 @@
             pltpu.VMEM((2, 4, 2, HEADS, 2, words, HEAD), bf16),
             pltpu.VMEM((rows, width), bf16),
             pltpu.VMEM((2, *heads), bf16),
-            pltpu.VMEM((2, *heads), bf16),
-            pltpu.VMEM((2, *heads), bf16),
+            pltpu.VMEM((2, 2, *heads), bf16),
             pltpu.VMEM(heads, bf16),
             pltpu.VMEM((2, 2, *heads), bf16),
-            pltpu.VMEM((2, 2, *heads), bf16),
-            pltpu.VMEM((2, 2, *heads), bf16),
+            pltpu.VMEM((2, 2, 2, *heads), bf16),
             pltpu.VMEM((2, *heads), bf16),
             pltpu.VMEM((2, *heads), bf16),
             pltpu.VMEM((2, 8, rows), f32),
@@ -497,11 +515,11 @@
             pltpu.SemaphoreType.DMA((2 * GROUP,)),
         ],
         compiler_params=pltpu.CompilerParams(
-            collective_id=0, has_side_effects=True, vmem_limit_bytes=60 << 20
+            collective_id=0, has_side_effects=True, vmem_limit_bytes=52 << 20
         ),
     )(
         query[0, 0], fresh_key[0, 0], fresh_value[0, 0], stale_kv[:, 0, 0], text_kv,
-        window, text_len,
+        window.T, text_len,
     )
     return result[None, None]
 

time: 68.4 us -> 55.1 us (0.81)
  the two profiles are of different devices: /device:TPU:3 before, /device:TPU:26 now
where the time goes in v6:
time: 55.1 us; the launch traced here: 55 us
  Pallas kernels  51.7 us (94%)
  local copies, waits for them, and re-layouts  2.58 us (5%)
  between operations  0.67 us (1%)
    pallas_call x1, Pallas kernels, on_device(): pl.pallas_call(kernel, out_shape=jax.ShapeDtypeStruct((rows, width), bf16...  51.7 us
    unnamed x5, local copies, waits for them, and re-layouts  2.58 us

profile of v6, /device:TPU:26, one launch (start us, length us, event | category | flops | bytes accessed | tf_op | source)
XLA Modules:
  0.0 55.0 jit_solution(7910608967992493215)
XLA Ops:
  0.7 0.0 copy-start
  0.7 0.9 %copy-done = bf16[2,16,1536]{2,1,0:T(8,128)(2,1)S(1)} copy-done((bf16[2,16,1536]{2,1,0:T(8,128)(2,1)S(1)}, bf16[2,16,1536]{2,1,0:T(8,128)(2,1)}, u32[]{:S(2)}) %copy-start) | copy-done | bytes 98328
  1.5 0.0 copy-start.1
  1.5 0.7 %copy-done.1 = s32[12,2]{0,1:T(2,128)S(1)} copy-done((s32[12,2]{0,1:T(2,128)S(1)}, s32[12,2]{0,1:T(2,128)}, u32[]{:S(2)}) %copy-start.1) | copy-done | bytes 120
  2.2 51.7 %shard_map.73 = bf16[384,1536]{1,0:T(8,128)(2,1)S(1)} custom-call(bf16[384,1536]{1,0:T(8,128)(2,1)} %bitcast.9, bf16[384,1536]{1,0:T(8,128)(2,1)} %bitcast.10, bf16[384,1536]{1,0:T(8,128)(2,1)} %bitcast.11, bf16[2,384,1536]{2,1,0:T(8,128)(2,1)} %bitcast.8, bf16[2,16,1536]{2,1,0:T(8,128)(2,1)S(1)} %copy-done, s32[2,12]{1,0:T(2,128)S(1)} %bitcast.7, ...), custom_call_target="tpu_custom_call" | custom-call | tf_op jit(solution)/shard_map/pallas_call | solution.py:480
  54.0 1.0 %copy.10 = bf16[1,1,384,1536]{3,2,1,0:T(8,128)(2,1)} copy(bf16[1,1,384,1536]{3,2,1,0:T(8,128)(2,1)S(1)} %bitcast.6) | data formatting | bytes 2359296
Async XLA Ops:
  0.7 0.9 %copy-start = (bf16[2,16,1536]{2,1,0:T(8,128)(2,1)S(1)}, bf16[2,16,1536]{2,1,0:T(8,128)(2,1)}, u32[]{:S(2)}) copy-start(bf16[2,16,1536]{2,1,0:T(8,128)(2,1)} %text.1) | copy-start | bytes 294916
  1.5 0.7 %copy-start.1 = (s32[12,2]{0,1:T(2,128)S(1)}, s32[12,2]{0,1:T(2,128)}, u32[]{:S(2)}) copy-start(s32[12,2]{0,1:T(2,128)} %param.12) | copy-start | bytes 292

commit v7 on v6

--- a/solution.py
+++ b/solution.py
@@ -38,7 +38,7 @@
     got11, got_sides, gotq,
     o_send, o_stat, o_got, o_got_stat,
     peak, total, mixed, done, order, place,
-    relay, load_sem, send_sem, recv_sem, text_send, text_recv, relay_send, relay_recv,
+    relay, hosted, load_sem, send_sem, recv_sem, text_send, text_recv, relay_send, relay_recv, hosted_send, hosted_recv,
 ):
     rows = q_all.shape[1]
     pack10, pack01 = sides.at[0], sides.at[1]
@@ -61,6 +61,19 @@
         jnp.logical_and(has_time[1], time != middle - 1),
     )
     bent = (time == middle, time == middle - 1)
+    loaded = jnp.logical_or(jnp.logical_or(time == 0, time == times - 1), inner)
+    inward = jnp.where(jnp.logical_or(time == 0, time == middle), time + 1, time - 1)
+    host = functools.reduce(
+        jnp.logical_or, [time == 1, time == middle - 2, time == middle + 1, time == times - 2]
+    )
+    guest = jnp.where(jnp.logical_or(time == 1, time == middle + 1), time - 1, time + 1)
+    crossing = (
+        jnp.logical_and(has_space[0], lax.rem(space, 4) == 0),
+        jnp.logical_and(has_space[1], lax.rem(space, 4) == 3),
+    )
+    hopping = [jnp.logical_and(loaded, crossing[d]) for d in (0, 1)]
+    hosting = [jnp.logical_and(host, crossing[d]) for d in (0, 1)]
+    direct = [jnp.logical_and(has_space[d], jnp.logical_not(hopping[d])) for d in (0, 1)]
     scale = math.log2(math.e) / math.sqrt(HEAD)
 
     mine = words.at[core, column, low]
@@ -97,8 +110,20 @@
         opposite = {"tm": 2 * middle - 1 - time, "space": partner_low}
         pl.semaphore_signal(barrier, inc=1, device_id=opposite, device_id_type=MESH)
 
+    for d in (0, 1):
+        @pl.when(hopping[d])
+        def _():
+            ahead = {"tm": inward, "space": space - 1 + 2 * d}
+            pl.semaphore_signal(barrier, inc=1, device_id=ahead, device_id_type=MESH)
+
+        @pl.when(hosting[d])
+        def _():
+            behind = {"tm": guest, "space": space - 1 + 2 * d}
+            pl.semaphore_signal(barrier, inc=1, device_id=behind, device_id_type=MESH)
+
     greeted = len(partners) + sum(has.astype(jnp.int32) for has in has_time + has_space)
     greeted = greeted + inner.astype(jnp.int32)
+    greeted = greeted + sum(hop.astype(jnp.int32) for hop in hopping + hosting)
 
     slots = slots_of(window)
     for head in range(HEADS):
@@ -201,7 +226,29 @@
                 detour(d, i).start()
 
     pack(pack01, 2 * GROUP)
-    send_both(has_space, along_space, 2, pack01, got01)
+    send_both(direct, along_space, 2, pack01, got01)
+
+    def hop(d, i):
+        kv, g = pieces[i]
+        return pltpu.make_async_remote_copy(
+            src_ref=pack01.at[kv, g], dst_ref=hosted.at[kv, g],
+            send_sem=send_sem.at[2, d], recv_sem=hosted_recv.at[i],
+            device_id={"tm": inward, "space": space - 1 + 2 * d}, device_id_type=MESH,
+        )
+
+    def home(d, i):
+        kv, g = pieces[i]
+        return pltpu.make_async_remote_copy(
+            src_ref=hosted.at[kv, g], dst_ref=got01.at[d, kv, g],
+            send_sem=hosted_send, recv_sem=recv_sem.at[2, d],
+            device_id={"tm": guest}, device_id_type=MESH,
+        )
+
+    for d in (0, 1):
+        @pl.when(hopping[d])
+        def _():
+            for i in range(len(pieces)):
+                hop(d, i).start()
 
     def rows_at(block):
         return pl.ds(block * ROW_BLOCK, ROW_BLOCK)
@@ -386,6 +433,13 @@
             along_space(4, d, o_send.at[d], o_got).start()
             along_space(5, d, o_stat.at[d], o_got_stat).start()
 
+    for d in (0, 1):
+        @pl.when(hosting[d])
+        def _():
+            for i in range(len(pieces)):
+                hop(d, i).wait_recv()
+                home(d, i).start()
+
     across.wait_recv()
     attend([
         job(own(3 * GROUP + g), [fresh(3 * GROUP + g), spoken(3 * GROUP + g)], finish(done, (3 * GROUP + g,)))
@@ -456,6 +510,10 @@
     @pl.when(inner)
     def _():
         pltpu.make_async_copy(relay, relay, relay_send).wait()
+
+    @pl.when(jnp.logical_or(*hosting))
+    def _():
+        pltpu.make_async_copy(hosted, hosted, hosted_send).wait()
 
     sent(has_space, along_space, 2, pack01, got01)
     sent(has_space, along_space, 3, packq, gotq)
@@ -506,11 +564,14 @@
             pltpu.SMEM((HEADS,), jnp.int32),
             pltpu.SMEM((HEADS,), jnp.int32),
             pltpu.VMEM((2, *heads), bf16),
+            pltpu.VMEM((2, *heads), bf16),
             pltpu.SemaphoreType.DMA((6,)),
             pltpu.SemaphoreType.DMA((6, 2)),
             pltpu.SemaphoreType.DMA((6, 2)),
             pltpu.SemaphoreType.DMA((5,)),
             pltpu.SemaphoreType.DMA((5,)),
+            pltpu.SemaphoreType.DMA(()),
+            pltpu.SemaphoreType.DMA((2 * GROUP,)),
             pltpu.SemaphoreType.DMA(()),
             pltpu.SemaphoreType.DMA((2 * GROUP,)),
         ],

time: 55.1 us -> 50.9 us (0.924)
  the two profiles are of different devices: /device:TPU:26 before, /device:TPU:233 now
where the time goes in v7:
time: 50.9 us; the launch traced here: 50.7 us
  Pallas kernels  47.5 us (93%)
  local copies, waits for them, and re-layouts  2.58 us (5%)
  between operations  0.67 us (1%)
    pallas_call x1, Pallas kernels, on_device(): pl.pallas_call(kernel, out_shape=jax.ShapeDtypeStruct((rows, width), bf16...  47.5 us
    unnamed x5, local copies, waits for them, and re-layouts  2.58 us

profile of v7, /device:TPU:233, one launch (start us, length us, event | category | flops | bytes accessed | tf_op | source)
XLA Modules:
  0.0 50.7 jit_solution(11672484051766187486)
XLA Ops:
  0.7 0.0 copy-start
  0.7 0.9 %copy-done = bf16[2,16,1536]{2,1,0:T(8,128)(2,1)S(1)} copy-done((bf16[2,16,1536]{2,1,0:T(8,128)(2,1)S(1)}, bf16[2,16,1536]{2,1,0:T(8,128)(2,1)}, u32[]{:S(2)}) %copy-start) | copy-done | bytes 98328
  1.5 0.0 copy-start.1
  1.5 0.7 %copy-done.1 = s32[12,2]{0,1:T(2,128)S(1)} copy-done((s32[12,2]{0,1:T(2,128)S(1)}, s32[12,2]{0,1:T(2,128)}, u32[]{:S(2)}) %copy-start.1) | copy-done | bytes 120
  2.2 47.5 %shard_map.73 = bf16[384,1536]{1,0:T(8,128)(2,1)S(1)} custom-call(bf16[384,1536]{1,0:T(8,128)(2,1)} %bitcast.9, bf16[384,1536]{1,0:T(8,128)(2,1)} %bitcast.10, bf16[384,1536]{1,0:T(8,128)(2,1)} %bitcast.11, bf16[2,384,1536]{2,1,0:T(8,128)(2,1)} %bitcast.8, bf16[2,16,1536]{2,1,0:T(8,128)(2,1)S(1)} %copy-done, s32[2,12]{1,0:T(2,128)S(1)} %bitcast.7, ...), custom_call_target="tpu_custom_call" | custom-call | tf_op jit(solution)/shard_map/pallas_call | solution.py:538
  49.7 1.0 %copy.10 = bf16[1,1,384,1536]{3,2,1,0:T(8,128)(2,1)} copy(bf16[1,1,384,1536]{3,2,1,0:T(8,128)(2,1)S(1)} %bitcast.6) | data formatting | bytes 2359296
Async XLA Ops:
  0.7 0.9 %copy-start = (bf16[2,16,1536]{2,1,0:T(8,128)(2,1)S(1)}, bf16[2,16,1536]{2,1,0:T(8,128)(2,1)}, u32[]{:S(2)}) copy-start(bf16[2,16,1536]{2,1,0:T(8,128)(2,1)} %text.1) | copy-start | bytes 294916
  1.5 0.7 %copy-start.1 = (s32[12,2]{0,1:T(2,128)S(1)}, s32[12,2]{0,1:T(2,128)}, u32[]{:S(2)}) copy-start(s32[12,2]{0,1:T(2,128)} %param.12) | copy-start | bytes 292

commit v8 on v7

--- a/solution.py
+++ b/solution.py
@@ -76,6 +76,42 @@
     direct = [jnp.logical_and(has_space[d], jnp.logical_not(hopping[d])) for d in (0, 1)]
     scale = math.log2(math.e) / math.sqrt(HEAD)
 
+    partner_low = column * 4 + (1 - low) * 2 + core
+    sibling = space + 1 - 2 * core
+    barrier = pltpu.get_barrier_semaphore()
+    for d in (0, 1):
+        @pl.when(has_time[d])
+        def _():
+            pl.semaphore_signal(barrier, inc=1, device_id={"tm": time - 1 + 2 * d}, device_id_type=MESH)
+
+        @pl.when(has_space[d])
+        def _():
+            pl.semaphore_signal(barrier, inc=1, device_id={"space": space - 1 + 2 * d}, device_id_type=MESH)
+
+    partners = [partner_low] + [lax.rem(space + 4 * d, spaces) for d in (1, 2, 3)]
+    for partner in partners:
+        pl.semaphore_signal(barrier, inc=1, device_id={"space": partner}, device_id_type=MESH)
+
+    @pl.when(inner)
+    def _():
+        opposite = {"tm": 2 * middle - 1 - time, "space": partner_low}
+        pl.semaphore_signal(barrier, inc=1, device_id=opposite, device_id_type=MESH)
+
+    for d in (0, 1):
+        @pl.when(hopping[d])
+        def _():
+            ahead = {"tm": inward, "space": space - 1 + 2 * d}
+            pl.semaphore_signal(barrier, inc=1, device_id=ahead, device_id_type=MESH)
+
+        @pl.when(hosting[d])
+        def _():
+            behind = {"tm": guest, "space": space - 1 + 2 * d}
+            pl.semaphore_signal(barrier, inc=1, device_id=behind, device_id_type=MESH)
+
+    greeted = len(partners) + sum(has.astype(jnp.int32) for has in has_time + has_space)
+    greeted = greeted + inner.astype(jnp.int32)
+    greeted = greeted + sum(hop.astype(jnp.int32) for hop in hopping + hosting)
+
     mine = words.at[core, column, low]
     lanes = [pl.ds(head * HEAD, HEAD) for head in range(HEADS)]
     for head, at in enumerate(lanes):
@@ -88,42 +124,6 @@
         pltpu.make_async_copy(target, target, load_sem.at[i])
         for i, target in enumerate((stale_all, q_all, mine, k_all, v_all))
     ]
-
-    partner_low = column * 4 + (1 - low) * 2 + core
-    sibling = space + 1 - 2 * core
-    barrier = pltpu.get_barrier_semaphore()
-    for d in (0, 1):
-        @pl.when(has_time[d])
-        def _():
-            pl.semaphore_signal(barrier, inc=1, device_id={"tm": time - 1 + 2 * d}, device_id_type=MESH)
-
-        @pl.when(has_space[d])
-        def _():
-            pl.semaphore_signal(barrier, inc=1, device_id={"space": space - 1 + 2 * d}, device_id_type=MESH)
-
-    partners = [partner_low] + [lax.rem(space + 4 * d, spaces) for d in (1, 2, 3)]
-    for partner in partners:
-        pl.semaphore_signal(barrier, inc=1, device_id={"space": partner}, device_id_type=MESH)
-
-    @pl.when(inner)
-    def _():
-        opposite = {"tm": 2 * middle - 1 - time, "space": partner_low}
-        pl.semaphore_signal(barrier, inc=1, device_id=opposite, device_id_type=MESH)
-
-    for d in (0, 1):
-        @pl.when(hopping[d])
-        def _():
-            ahead = {"tm": inward, "space": space - 1 + 2 * d}
-            pl.semaphore_signal(barrier, inc=1, device_id=ahead, device_id_type=MESH)
-
-        @pl.when(hosting[d])
-        def _():
-            behind = {"tm": guest, "space": space - 1 + 2 * d}
-            pl.semaphore_signal(barrier, inc=1, device_id=behind, device_id_type=MESH)
-
-    greeted = len(partners) + sum(has.astype(jnp.int32) for has in has_time + has_space)
-    greeted = greeted + inner.astype(jnp.int32)
-    greeted = greeted + sum(hop.astype(jnp.int32) for hop in hopping + hosting)
 
     slots = slots_of(window)
     for head in range(HEADS):
@@ -327,6 +327,13 @@
 
         return after
 
+    def both_of(first, second):
+        def after(*result):
+            first(*result)
+            second(*result)
+
+        return after
+
     def fresh(slot):
         head = order[slot]
         return k_all[head], v_all[head], None, None
@@ -337,11 +344,22 @@
         values = words[:, :, :, head, 1].reshape(count, HEAD)
         return keys, values, live, None
 
-    def near(got, g, has):
-        return [(got[e, 0, g], got[e, 1, g], None, has[e]) for e in (0, 1)]
-
     def side_ok(d, position, count):
         return jnp.where(d == 0, position > 0, position < count - 1)
+
+    soon_time = jnp.logical_or(time == middle, time == 0).astype(jnp.int32)
+    outer = jnp.logical_or(time == 0, time == times - 1)
+    soon_space = 1 - core
+    ok_time = functools.partial(side_ok, position=time, count=times)
+    ok_space = functools.partial(side_ok, position=space, count=spaces)
+
+    def arrived_one(ok, make, kind, d, source, target):
+        @pl.when(ok(d))
+        def _():
+            make(kind, 1 - d, source, target).wait_recv()
+
+    def beside(got, g, d, ok):
+        return got[d, 0, g], got[d, 1, g], None, ok(d)
 
     count = 2 * spaces // 2 * words.shape[5]
     index = lax.broadcasted_iota(jnp.int32, (1, count), 1)
@@ -390,6 +408,13 @@
             along_time(0, d, pack11, got11).wait_send()
             along_time(1, d, pack10, got10).start()
 
+    for d in (0, 1):
+        @pl.when(bent[d])
+        def _():
+            for i in range(len(pieces)):
+                detour(d, i).wait_recv()
+                onward(d, i).start()
+
     for copy in spread:
         copy.wait_recv()
     half = words.at[core]
@@ -399,39 +424,38 @@
     )
     across.start()
 
-    for d in (0, 1):
-        @pl.when(bent[d])
-        def _():
-            for i in range(len(pieces)):
-                detour(d, i).wait_recv()
-                onward(d, i).start()
-
-    arrived(has_time, along_time, 0, pack11, got11)
+    arrived_one(ok_time, along_time, 0, soon_time, pack11, got11)
     lane = lax.broadcasted_iota(jnp.int32, (rows, LANES), 1)
 
-    @pl.loop(0, 2)
-    def _(i):
-        d = lax.rem(i + core, 2)
-
-        @pl.when(side_ok(d, space, spaces))
-        def _():
-            def give(g):
-                def after(here, top, weight, value):
-                    o_send[d, g, here] = (value / weight).astype(jnp.bfloat16)
-                    peak[g][3 + d, here] = top + jnp.log2(weight)
-
-                return after
-
-            attend([
-                job(visitor(d, g), near(got11, g, has_time), give(g), saved(g, 3 + d))
-                for g in range(GROUP)
-            ])
-            stats = jnp.zeros((rows, LANES), jnp.float32)
-            for g in range(GROUP):
-                stats = jnp.where(lane == g, peak[g][3 + d], stats)
-            o_stat[d] = stats.T[:8]
-            along_space(4, d, o_send.at[d], o_got).start()
-            along_space(5, d, o_stat.at[d], o_got_stat).start()
+    arrived_one(ok_time, along_time, 0, 1 - soon_time, pack11, got11)
+
+    def answer(frames):
+        @pl.loop(0, 2)
+        def _(i):
+            d = lax.rem(i + core, 2)
+
+            @pl.when(side_ok(d, space, spaces))
+            def _():
+                def give(g):
+                    def after(here, top, weight, value):
+                        o_send[d, g, here] = (value / weight).astype(jnp.bfloat16)
+                        peak[g][3 + d, here] = top + jnp.log2(weight)
+
+                    return after
+
+                attend([
+                    job(visitor(d, g), [beside(got11, g, e, ok_time) for e in frames], give(g), saved(g, 3 + d))
+                    for g in range(GROUP)
+                ])
+                stats = jnp.zeros((rows, LANES), jnp.float32)
+                for g in range(GROUP):
+                    stats = jnp.where(lane == g, peak[g][3 + d], stats)
+                o_stat[d] = stats.T[:8]
+                along_space(4, d, o_send.at[d], o_got).start()
+                along_space(5, d, o_stat.at[d], o_got_stat).start()
+
+    pl.when(outer)(lambda: answer((soon_time,)))
+    pl.when(jnp.logical_not(outer))(lambda: answer((0, 1)))
 
     for d in (0, 1):
         @pl.when(hosting[d])
@@ -446,35 +470,59 @@
         for g in range(GROUP)
     ])
 
-    attend([
-        job(own(g), [spoken(g), *near(got11, g, has_time)], save(g, 0), saved(g, 0))
-        for g in range(GROUP)
-    ])
-    outer = jnp.logical_or(time == 0, time == times - 1)
+    def own_both(frames):
+        attend([
+            job(own(g), [spoken(g)] + [beside(got11, g, e, ok_time) for e in frames], save(g, 0), saved(g, 0))
+            for g in range(GROUP)
+        ])
+
+    pl.when(outer)(lambda: own_both((soon_time,)))
+    pl.when(jnp.logical_not(outer))(lambda: own_both((0, 1)))
+    def side(k, soon):
+        first = jnp.where(k == 0, soon_time, soon_space)
+        return first if soon else 1 - first
+
+    def arrived_side(k, d):
+        @pl.when(k == 0)
+        def _():
+            arrived_one(ok_time, along_time, 1, d, pack10, got10)
+
+        @pl.when(k == 1)
+        def _():
+            arrived_one(ok_space, along_space, 2, d, pack01, got01)
+
+    def beside_of(k, g, d):
+        ok = jnp.where(k == 0, ok_time(d), ok_space(d))
+        return got_sides[k, d, 0, g], got_sides[k, d, 1, g], None, ok
+
+    @pl.loop(0, 2)
+    def _(i):
+        k = 1 - i
+        d = side(k, True)
+        arrived_side(k, d)
+        attend([
+            job(
+                own((1 + k) * GROUP + g), [spoken((1 + k) * GROUP + g), beside_of(k, g, d)],
+                both_of(save(g, 1 + k), finish(done, ((1 + k) * GROUP + g,))), saved(g, 1 + k),
+            )
+            for g in range(GROUP)
+        ])
 
     @pl.loop(0, 2)
     def _(i):
         k = jnp.where(outer, i, 1 - i)
-
-        @pl.when(k == 0)
-        def _():
-            arrived(has_time, along_time, 1, pack10, got10)
-
-        @pl.when(k == 1)
-        def _():
-            arrived(has_space, along_space, 2, pack01, got01)
-
-        valid = [jnp.where(k == 0, has_time[e], has_space[e]) for e in (0, 1)]
-        attend([
-            job(
-                own((1 + k) * GROUP + g),
-                [spoken((1 + k) * GROUP + g)]
-                + [(got_sides[k, e, 0, g], got_sides[k, e, 1, g], None, valid[e]) for e in (0, 1)],
-                finish(done, ((1 + k) * GROUP + g,)),
-                saved(g, 1 + k),
-            )
-            for g in range(GROUP)
-        ])
+        d = side(k, False)
+        arrived_side(k, d)
+
+        @pl.when(jnp.where(k == 0, ok_time(d), ok_space(d)))
+        def _():
+            attend([
+                job(
+                    own((1 + k) * GROUP + g), [beside_of(k, g, d)],
+                    finish(done, ((1 + k) * GROUP + g,)), saved(g, 1 + k),
+                )
+                for g in range(GROUP)
+            ])
 
     logs = []
     for d in (0, 1):

time: 50.9 us -> 49.9 us (0.980)
  the two profiles are of different devices: /device:TPU:233 before, /device:TPU:2 now
where the time goes in v8:
time: 49.9 us; the launch traced here: 49.8 us
  Pallas kernels  46.5 us (93%)
  local copies, waits for them, and re-layouts  2.58 us (5%)
  between operations  0.67 us (1%)
    pallas_call x1, Pallas kernels, on_device(): pl.pallas_call(kernel, out_shape=jax.ShapeDtypeStruct((rows, width), bf16...  46.5 us
    unnamed x5, local copies, waits for them, and re-layouts  2.58 us

profile of v8, /device:TPU:2, one launch (start us, length us, event | category | flops | bytes accessed | tf_op | source)
XLA Modules:
  0.0 49.8 jit_solution(3054392628919445952)
XLA Ops:
  0.7 0.0 copy-start
  0.7 0.9 %copy-done = bf16[2,16,1536]{2,1,0:T(8,128)(2,1)S(1)} copy-done((bf16[2,16,1536]{2,1,0:T(8,128)(2,1)S(1)}, bf16[2,16,1536]{2,1,0:T(8,128)(2,1)}, u32[]{:S(2)}) %copy-start) | copy-done | bytes 98328
  1.5 0.0 copy-start.1
  1.5 0.7 %copy-done.1 = s32[12,2]{0,1:T(2,128)S(1)} copy-done((s32[12,2]{0,1:T(2,128)S(1)}, s32[12,2]{0,1:T(2,128)}, u32[]{:S(2)}) %copy-start.1) | copy-done | bytes 120
  2.2 46.5 %shard_map.73 = bf16[384,1536]{1,0:T(8,128)(2,1)S(1)} custom-call(bf16[384,1536]{1,0:T(8,128)(2,1)} %bitcast.9, bf16[384,1536]{1,0:T(8,128)(2,1)} %bitcast.10, bf16[384,1536]{1,0:T(8,128)(2,1)} %bitcast.11, bf16[2,384,1536]{2,1,0:T(8,128)(2,1)} %bitcast.8, bf16[2,16,1536]{2,1,0:T(8,128)(2,1)S(1)} %copy-done, s32[2,12]{1,0:T(2,128)S(1)} %bitcast.7, ...), custom_call_target="tpu_custom_call" | custom-call | tf_op jit(solution)/shard_map/pallas_call | solution.py:586
  48.7 1.0 %copy.10 = bf16[1,1,384,1536]{3,2,1,0:T(8,128)(2,1)} copy(bf16[1,1,384,1536]{3,2,1,0:T(8,128)(2,1)S(1)} %bitcast.6) | data formatting | bytes 2359296
Async XLA Ops:
  0.7 0.9 %copy-start = (bf16[2,16,1536]{2,1,0:T(8,128)(2,1)S(1)}, bf16[2,16,1536]{2,1,0:T(8,128)(2,1)}, u32[]{:S(2)}) copy-start(bf16[2,16,1536]{2,1,0:T(8,128)(2,1)} %text.1) | copy-start | bytes 294916
  1.5 0.7 %copy-start.1 = (s32[12,2]{0,1:T(2,128)S(1)}, s32[12,2]{0,1:T(2,128)}, u32[]{:S(2)}) copy-start(s32[12,2]{0,1:T(2,128)} %param.12) | copy-start | bytes 292

commit v9 on v8

--- a/solution.py
+++ b/solution.py
@@ -186,15 +186,19 @@
     loads[2].wait()
     pl.semaphore_wait(barrier, greeted)
     swap.start()
+    def spread_text():
+        swap.wait_recv()
+        for copy in spread:
+            copy.start()
+
+    pl.when(loaded)(spread_text)
     loads[0].wait()
     pack(pack11, 0)
     send_both(has_time, along_time, 0, pack11, got11)
     for head, at in enumerate(lanes):
         pltpu.make_async_copy(fresh_key.at[:, at], k_all.at[head], load_sem.at[3]).start()
         pltpu.make_async_copy(fresh_value.at[:, at], v_all.at[head], load_sem.at[4]).start()
-    swap.wait_recv()
-    for copy in spread:
-        copy.start()
+    pl.when(jnp.logical_not(loaded))(spread_text)
     loads[1].wait()
     for g in range(GROUP):
         packq[g] = q_all[order[g]]

time: 49.9 us -> 51 us (1.022)
  the two profiles are of different devices: /device:TPU:2 before, /device:TPU:50 now
where the time goes in v9:
time: 51 us; the launch traced here: 50.8 us
  Pallas kernels  47.6 us (93%)
  local copies, waits for them, and re-layouts  2.58 us (5%)
  between operations  0.67 us (1%)
    pallas_call x1, Pallas kernels, on_device(): pl.pallas_call(kernel, out_shape=jax.ShapeDtypeStruct((rows, width), bf16...  47.6 us
    unnamed x5, local copies, waits for them, and re-layouts  2.58 us

profile of v9, /device:TPU:50, one launch (start us, length us, event | category | flops | bytes accessed | tf_op | source)
XLA Modules:
  0.0 50.8 jit_solution(942027724436215604)
XLA Ops:
  0.7 0.0 copy-start
  0.7 0.9 %copy-done = bf16[2,16,1536]{2,1,0:T(8,128)(2,1)S(1)} copy-done((bf16[2,16,1536]{2,1,0:T(8,128)(2,1)S(1)}, bf16[2,16,1536]{2,1,0:T(8,128)(2,1)}, u32[]{:S(2)}) %copy-start) | copy-done | bytes 98328
  1.5 0.0 copy-start.1
  1.5 0.7 %copy-done.1 = s32[12,2]{0,1:T(2,128)S(1)} copy-done((s32[12,2]{0,1:T(2,128)S(1)}, s32[12,2]{0,1:T(2,128)}, u32[]{:S(2)}) %copy-start.1) | copy-done | bytes 120
  2.2 47.6 %shard_map.73 = bf16[384,1536]{1,0:T(8,128)(2,1)S(1)} custom-call(bf16[384,1536]{1,0:T(8,128)(2,1)} %bitcast.9, bf16[384,1536]{1,0:T(8,128)(2,1)} %bitcast.10, bf16[384,1536]{1,0:T(8,128)(2,1)} %bitcast.11, bf16[2,384,1536]{2,1,0:T(8,128)(2,1)} %bitcast.8, bf16[2,16,1536]{2,1,0:T(8,128)(2,1)S(1)} %copy-done, s32[2,12]{1,0:T(2,128)S(1)} %bitcast.7, ...), custom_call_target="tpu_custom_call" | custom-call | tf_op jit(solution)/shard_map/pallas_call | solution.py:590
  49.8 1.0 %copy.10 = bf16[1,1,384,1536]{3,2,1,0:T(8,128)(2,1)} copy(bf16[1,1,384,1536]{3,2,1,0:T(8,128)(2,1)S(1)} %bitcast.6) | data formatting | bytes 2359296
Async XLA Ops:
  0.7 0.9 %copy-start = (bf16[2,16,1536]{2,1,0:T(8,128)(2,1)S(1)}, bf16[2,16,1536]{2,1,0:T(8,128)(2,1)}, u32[]{:S(2)}) copy-start(bf16[2,16,1536]{2,1,0:T(8,128)(2,1)} %text.1) | copy-start | bytes 294916
  1.5 0.7 %copy-start.1 = (s32[12,2]{0,1:T(2,128)S(1)}, s32[12,2]{0,1:T(2,128)}, u32[]{:S(2)}) copy-start(s32[12,2]{0,1:T(2,128)} %param.12) | copy-start | bytes 292
